TPU v7x, 128 devices: a whole 4x4x4 slice. The times are simulated.
128 devices in a mesh: dp: 16 (over x, y), ctx: 8 (over z, core).
Axes of the slice: x: 4, y: 4, z: 4, core: 2. Of those that a mesh axis runs over, the one named last changes fastest.
Arguments:
- queries: bfloat16 [24576, 4096], P(('dp', 'ctx'))
- keys: bfloat16 [24576, 512], P(('dp', 'ctx'))
- values: bfloat16 [24576, 512], P(('dp', 'ctx')), may hold values from -6 to 6
- grad_out: bfloat16 [24576, 4096], P(('dp', 'ctx')), may hold values from -6 to 6
- destination: int32 [24576], P(('dp', 'ctx')), may hold values from 0 to 24575, as said below
- lengths: int32 [16, 2], replicated, may hold values from 1 to 1024, 1536 in all within a row
Outputs:
- attended: bfloat16 [24576, 4096], P(('dp', 'ctx'))
- grad_queries: bfloat16 [24576, 4096], P(('dp', 'ctx'))
- grad_keys: bfloat16 [24576, 512], P(('dp', 'ctx'))
- grad_values: bfloat16 [24576, 512], P(('dp', 'ctx'))
Inputs may be any that keep to these rules, and one draw needn't show every extreme that they name: destination is a permutation of all rows; a row keeps its index of ctx; every device of a group receives exactly 192 rows; the rows of one device going to one index of dp number at most 24, and that many in every draw. Each group's lengths sum to 1536.
All inputs are finite; a program needn't handle non-finite values.
Results may differ from a plain program's by a relative error of at most 0.012.
The roundings to bfloat16 on the way count: a program that leaves them out, or rounds other values in their place, can miss the bound.
Values may be sent and summed in bfloat16 or wider, within the bound.
A program may use at most 256 MiB of HBM per device.

v0:
```python
import jax
import jax.numpy as jnp
from jax import lax
from jax.sharding import PartitionSpec as P

D_HEAD = 128


def local(queries, keys, values, grad_out, destination, lengths):
    n_dp = lax.axis_size("dp")
    n_ctx = lax.axis_size("ctx")
    tok = queries.shape[0]
    cap = 2 * tok // n_dp
    width_q = queries.shape[1]
    width_kv = keys.shape[1]
    kv_count = width_kv // D_HEAD
    ratio = width_q // D_HEAD // kv_count
    scale = 1.0 / D_HEAD**0.5
    group_of = destination // (n_ctx * tok)
    place = destination % tok
    onehot = (group_of[:, None] == jnp.arange(n_dp, dtype=jnp.int32)[None, :]).astype(jnp.int32)
    rank = jnp.sum(jnp.cumsum(onehot, axis=0) * onehot, axis=1) - 1
    slot_of = group_of * cap + rank
    source = (
        jnp.full((n_dp * cap,), tok, jnp.int32).at[slot_of].set(jnp.arange(tok, dtype=jnp.int32))
    )
    filled = source < tok

    def to_slots(rows):
        padded = jnp.concatenate([rows, jnp.zeros((1, rows.shape[1]), rows.dtype)], axis=0)
        return padded[source].reshape(n_dp, cap, rows.shape[1])

    sent_place = jnp.where(filled, place[jnp.minimum(source, tok - 1)], -1).reshape(n_dp, cap)
    got_place = lax.all_to_all(sent_place, "dp", split_axis=0, concat_axis=0, tiled=True)
    got_q, got_k, got_v, got_d = (
        lax.all_to_all(to_slots(queries), "dp", split_axis=0, concat_axis=0, tiled=True),
        lax.all_to_all(to_slots(keys), "dp", split_axis=0, concat_axis=0, tiled=True),
        lax.all_to_all(to_slots(values), "dp", split_axis=0, concat_axis=0, tiled=True),
        lax.all_to_all(to_slots(grad_out), "dp", split_axis=0, concat_axis=0, tiled=True),
    )
    flat_place = got_place.reshape(-1)
    pick = (
        jnp.zeros((tok,), jnp.int32)
        .at[jnp.where(flat_place >= 0, flat_place, tok)]
        .set(jnp.arange(n_dp * cap, dtype=jnp.int32), mode="drop")
    )
    q_local = got_q.reshape(n_dp * cap, width_q)[pick]
    k_local = got_k.reshape(n_dp * cap, width_kv)[pick]
    v_local = got_v.reshape(n_dp * cap, width_kv)[pick]
    d_local = got_d.reshape(n_dp * cap, width_q)[pick]

    def to_owners(rows):
        return rows[jnp.maximum(flat_place, 0)].reshape(n_dp, cap, rows.shape[1])

    def read_back(returned):
        return returned.reshape(n_dp * cap, -1)[slot_of]

    member = lax.axis_index("ctx")
    group = lax.axis_index("dp")
    group_rows = tok * n_ctx
    seq_len = lax.dynamic_index_in_dim(lengths, group, 0, keepdims=False)
    ends = jnp.cumsum(seq_len)
    key_pos = jnp.arange(group_rows, dtype=jnp.int32)
    key_seg = jnp.sum((key_pos[:, None] >= ends[None, :]).astype(jnp.int32), axis=1)
    query_pos = member * tok + jnp.arange(tok, dtype=jnp.int32)
    query_seg = jnp.sum((query_pos[:, None] >= ends[None, :]).astype(jnp.int32), axis=1)
    allowed = (query_seg[:, None] == key_seg[None, :]) & (query_pos[:, None] >= key_pos[None, :])
    k_all, v_all = (
        lax.all_gather(k_local, "ctx", axis=0, tiled=True),
        lax.all_gather(v_local, "ctx", axis=0, tiled=True),
    )
    q_heads = q_local.reshape(tok, kv_count, ratio, D_HEAD)
    d_heads = d_local.reshape(tok, kv_count, ratio, D_HEAD)
    q_groups = jnp.transpose(q_heads, (1, 0, 2, 3))
    d_groups = jnp.transpose(d_heads, (1, 0, 2, 3))

    def forward_group(items):
        q_one, k_one, v_one = items
        scores = jnp.einsum("qrd,kd->rqk", q_one, k_one, preferred_element_type=jnp.float32) * scale
        masked = jnp.where(allowed[None], scores, -jnp.inf)
        top = jnp.max(masked, axis=-1, keepdims=True)
        expo = jnp.exp(masked - top)
        prob = expo / jnp.sum(expo, axis=-1, keepdims=True)
        att = jnp.einsum(
            "rqk,kd->qrd", prob.astype(jnp.bfloat16), v_one, preferred_element_type=jnp.float32
        ).astype(jnp.bfloat16)
        return (prob, att)

    k_groups = jnp.transpose(k_all.reshape(group_rows, kv_count, D_HEAD), (1, 0, 2))
    v_groups = jnp.transpose(v_all.reshape(group_rows, kv_count, D_HEAD), (1, 0, 2))
    prob_all, att_all = lax.map(forward_group, (q_groups, k_groups, v_groups))
    attended_rows = jnp.transpose(att_all, (1, 0, 2, 3)).reshape(tok, width_q)

    def backward_group(items):
        prob, d_one, att, k_one, v_one = items
        delta = jnp.sum(d_one.astype(jnp.float32) * att.astype(jnp.float32), axis=-1)
        dprob = jnp.einsum("qrd,kd->rqk", d_one, v_one, preferred_element_type=jnp.float32)
        dscore = prob * (dprob - jnp.transpose(delta, (1, 0))[..., None])
        dscore_b = dscore.astype(jnp.bfloat16)
        grad_q = (
            jnp.einsum("rqk,kd->qrd", dscore_b, k_one, preferred_element_type=jnp.float32) * scale
        ).astype(jnp.bfloat16)
        return (dscore_b, grad_q)

    dscore_b, grad_q_all = lax.map(
        backward_group, (prob_all, d_groups, att_all, k_groups, v_groups)
    )
    prob_b = prob_all.astype(jnp.bfloat16)
    grad_q = jnp.transpose(grad_q_all, (1, 0, 2, 3)).reshape(tok, width_q)
    grad_k_part = (
        jnp.einsum("grqk,qgrd->kgd", dscore_b, q_heads, preferred_element_type=jnp.float32) * scale
    )
    grad_v_part = jnp.einsum("grqk,qgrd->kgd", prob_b, d_heads, preferred_element_type=jnp.float32)
    key_grads = lax.psum_scatter(
        jnp.concatenate(
            [
                grad_k_part.reshape(lax.axis_size("ctx") * tok, width_kv),
                grad_v_part.reshape(lax.axis_size("ctx") * tok, width_kv),
            ],
            axis=1,
        ),
        "ctx",
        scatter_dimension=0,
        tiled=True,
    )
    grad_k = key_grads[:, :width_kv].astype(jnp.bfloat16)
    grad_v = key_grads[:, width_kv:].astype(jnp.bfloat16)
    back_o, back_q, back_k, back_v = (
        lax.all_to_all(to_owners(attended_rows), "dp", split_axis=0, concat_axis=0, tiled=True),
        lax.all_to_all(to_owners(grad_q), "dp", split_axis=0, concat_axis=0, tiled=True),
        lax.all_to_all(to_owners(grad_k), "dp", split_axis=0, concat_axis=0, tiled=True),
        lax.all_to_all(to_owners(grad_v), "dp", split_axis=0, concat_axis=0, tiled=True),
    )
    return (read_back(back_o), read_back(back_q), read_back(back_k), read_back(back_v))


def solution(mesh):
    placed = (
        P(("dp", "ctx"), None),
        P(("dp", "ctx"), None),
        P(("dp", "ctx"), None),
        P(("dp", "ctx"), None),
        P(("dp", "ctx")),
        P(),
    )
    return jax.shard_map(
        local,
        mesh=mesh,
        in_specs=placed,
        out_specs=(
            P(("dp", "ctx"), None),
            P(("dp", "ctx"), None),
            P(("dp", "ctx"), None),
            P(("dp", "ctx"), None),
        ),
        check_vma=False,
    )
```

profile of v0, /device:TPU:16, one launch (start us, length us, event | category | flops | bytes accessed | tf_op | source)
XLA Modules:
  0.0 490.5 jit_solution(8495102083871710180)
XLA Ops:
  10.1 2.8 gather_fusion.1
  13.7 7.3 %all-to-all-start.1 = ((s32[16,1,24]{2,1,0:T(1,128)}), s32[16,1,24]{2,1,0:T(1,128)S(1)}, u32[]{:S(2)}, u32[]{:S(2)}) async-start(s32[16,1,24]{2,1,0:T(1,128)} %all_to_all.31), calls=%async_computation.1 | async-start | bytes 16384 | tf_op jit(solution)/shard_map/all_to_all | solution.py:34
  21.9 2.6 gather_fusion.5
  26.2 5.7 %all-to-all-start.3 = ((bf16[16,24,512]{2,1,0:T(8,128)(2,1)}), bf16[16,24,512]{2,1,0:T(8,128)(2,1)S(1)}, u32[]{:S(2)}, u32[]{:S(2)}) async-start(bf16[16,24,512]{2,1,0:T(8,128)(2,1)} %bitcast.19), calls=%async_computation.3 | async-start | bytes 786432 | tf_op jit(solution)/shard_map/all_to_all | solution.py:38
  31.9 2.6 gather_fusion
  34.5 4.6 all-to-all-done.3
  39.1 5.7 %all-to-all-start = ((bf16[16,24,512]{2,1,0:T(8,128)(2,1)}), bf16[16,24,512]{2,1,0:T(8,128)(2,1)S(1)}, u32[]{:S(2)}, u32[]{:S(2)}) async-start(bf16[16,24,512]{2,1,0:T(8,128)(2,1)} %bitcast.13), calls=%async_computation | async-start | bytes 786432 | tf_op jit(solution)/shard_map/all_to_all | solution.py:37
  46.4 4.0 gather_fusion.3
  52.0 6.3 %all-to-all-start.2 = ((bf16[16,24,4096]{2,1,0:T(8,128)(2,1)}), bf16[16,24,4096]{2,1,0:T(8,128)(2,1)}, u32[]{:S(2)}, u32[]{:S(2)}) async-start(bf16[16,24,4096]{2,1,0:T(8,128)(2,1)} %bitcast.205), calls=%async_computation.2 | async-start | bytes 6291456 | tf_op jit(solution)/shard_map/all_to_all | solution.py:36
  60.2 2.9 scatter_custom_fusion.1
  66.4 4.0 gather_fusion.9
  70.4 24.9 %all-to-all-done.2 = bf16[16,24,4096]{2,1,0:T(8,128)(2,1)} async-done(((bf16[16,24,4096]{2,1,0:T(8,128)(2,1)}), bf16[16,24,4096]{2,1,0:T(8,128)(2,1)}, u32[]{:S(2)}, u32[]{:S(2)}) %all-to-all-start.2) | async-done | bytes 3145760 | tf_op jit(solution)/shard_map/all_to_all | solution.py:36
  95.4 6.4 %all-to-all-start.5 = ((bf16[16,24,4096]{2,1,0:T(8,128)(2,1)}), bf16[16,24,4096]{2,1,0:T(8,128)(2,1)S(1)}, u32[]{:S(2)}, u32[]{:S(2)}) async-start(bf16[16,24,4096]{2,1,0:T(8,128)(2,1)} %bitcast.204), calls=%async_computation.5 | async-start | bytes 6291456 | tf_op jit(solution)/shard_map/all_to_all | solution.py:39
  104.3 6.5 %gather_fusion.4 = bf16[192,4096]{1,0:T(8,128)(2,1)} fusion(bf16[384,4096]{1,0:T(8,128)(2,1)} %bitcast.17, s32[1024]{0:T(1024)S(1)} %pad_clamp_fusion.2), kind=kCustom, calls=%fused_computation.4 | custom fusion | bytes 3146496 | tf_op jit(solution)/shard_map/gather | solution.py:47
  110.8 2.9 copy.54
  113.7 3.2 copy.72
  116.8 23.4 %all-to-all-done.5 = bf16[16,24,4096]{2,1,0:T(8,128)(2,1)S(1)} async-done(((bf16[16,24,4096]{2,1,0:T(8,128)(2,1)}), bf16[16,24,4096]{2,1,0:T(8,128)(2,1)S(1)}, u32[]{:S(2)}, u32[]{:S(2)}) %all-to-all-start.5) | async-done | bytes 3145760 | tf_op jit(solution)/shard_map/all_to_all | solution.py:39
  140.2 2.7 gather_fusion.10
  146.4 2.9 bitcast_bitcast_fusion
  149.3 2.8 bitcast_bitcast_fusion.1
  152.5 79.9 %while.26 = (s32[]{:T(128)}, f32[4,8,192,1536]{3,2,1,0:T(8,128)}, bf16[4,192,8,128]{3,1,2,0:T(8,128)(2,1)S(1)}, bf16[4,1536,128]{2,1,0:T(8,128)(2,1)}, bf16[4,19...) while((s32[]{:T(128)}, f32[4,8,192,1536]{3,2,1,0:T(8,128)}, ...), condition=%wide.region_11.12_spmd.clone, body=%wide.region_8.11_spmd.clone.sunk | while | flops 1225557504 | bytes 77691008 | solution.py:91
  153.2 8.0 %fusion.116 = (f32[8,192]{1,0:T(8,128)S(1)}, f32[8,192,1536]{2,1,0:T(8,128)}) fusion(pred[192,1536]{1,0:T(8,128)(4,1)S(1)} %fusion.115, bf16[4,192,8,128]{3,1,2,0:T(8,128)(2,1)} %get-tuple-element.288, s32[]{:T(128)} %get-tuple-element.274, bf16[4,1536,128]{2,1,0:T(8,128)(2,1)} %get-tuple-element.287), kind=kOutput, calls=%fused_computation.117.clone.1 | convolution fusion | flops 613418496 | bytes 10525696 | tf_op jit(solution)/shard_map/while/body/eval_jaxpr/sub | solution.py:82
  161.2 8.8 %bitcast_dynamic-update-slice_fusion.2 = f32[4,8,192,1536]{3,2,1,0:T(8,128)} fusion(f32[4,8,192,1536]{3,2,1,0:T(8,128)} %get-tuple-element.275, s32[]{:T(128)} %get-tuple-element.274, f32[8,192,1536]{2,1,0:T(8,128)} %get-tuple-element.262, f32[8,192]{1,0:T(8,128)S(1)} %get-tuple-element.263), kind=kLoop, calls=%fused_computation.39.clone.1 | loop fusion | flops 2359296 | bytes 18881024 | tf_op jit(solution)/shard_map/while/body/jit(dynamic_update_index_in_dim)/dynamic_update_slice | solution.py:91
  170.0 2.6 fusion.117
  173.1 8.0 %fusion.116 = (f32[8,192]{1,0:T(8,128)S(1)}, f32[8,192,1536]{2,1,0:T(8,128)}) fusion(pred[192,1536]{1,0:T(8,128)(4,1)S(1)} %fusion.115, bf16[4,192,8,128]{3,1,2,0:T(8,128)(2,1)} %get-tuple-element.288, s32[]{:T(128)} %get-tuple-element.274, bf16[4,1536,128]{2,1,0:T(8,128)(2,1)} %get-tuple-element.287), kind=kOutput, calls=%fused_computation.117.clone.1 | convolution fusion | flops 613418496 | bytes 10525696 | tf_op jit(solution)/shard_map/while/body/eval_jaxpr/sub | solution.py:82
  181.1 8.8 %bitcast_dynamic-update-slice_fusion.2 = f32[4,8,192,1536]{3,2,1,0:T(8,128)} fusion(f32[4,8,192,1536]{3,2,1,0:T(8,128)} %get-tuple-element.275, s32[]{:T(128)} %get-tuple-element.274, f32[8,192,1536]{2,1,0:T(8,128)} %get-tuple-element.262, f32[8,192]{1,0:T(8,128)S(1)} %get-tuple-element.263), kind=kLoop, calls=%fused_computation.39.clone.1 | loop fusion | flops 2359296 | bytes 18881024 | tf_op jit(solution)/shard_map/while/body/jit(dynamic_update_index_in_dim)/dynamic_update_slice | solution.py:91
  189.9 2.6 fusion.117
  193.0 8.0 %fusion.116 = (f32[8,192]{1,0:T(8,128)S(1)}, f32[8,192,1536]{2,1,0:T(8,128)}) fusion(pred[192,1536]{1,0:T(8,128)(4,1)S(1)} %fusion.115, bf16[4,192,8,128]{3,1,2,0:T(8,128)(2,1)} %get-tuple-element.288, s32[]{:T(128)} %get-tuple-element.274, bf16[4,1536,128]{2,1,0:T(8,128)(2,1)} %get-tuple-element.287), kind=kOutput, calls=%fused_computation.117.clone.1 | convolution fusion | flops 613418496 | bytes 10525696 | tf_op jit(solution)/shard_map/while/body/eval_jaxpr/sub | solution.py:82
  201.0 8.9 %bitcast_dynamic-update-slice_fusion.2 = f32[4,8,192,1536]{3,2,1,0:T(8,128)} fusion(f32[4,8,192,1536]{3,2,1,0:T(8,128)} %get-tuple-element.275, s32[]{:T(128)} %get-tuple-element.274, f32[8,192,1536]{2,1,0:T(8,128)} %get-tuple-element.262, f32[8,192]{1,0:T(8,128)S(1)} %get-tuple-element.263), kind=kLoop, calls=%fused_computation.39.clone.1 | loop fusion | flops 2359296 | bytes 18881024 | tf_op jit(solution)/shard_map/while/body/jit(dynamic_update_index_in_dim)/dynamic_update_slice | solution.py:91
  209.9 2.6 fusion.117
  213.0 8.0 %fusion.116 = (f32[8,192]{1,0:T(8,128)S(1)}, f32[8,192,1536]{2,1,0:T(8,128)}) fusion(pred[192,1536]{1,0:T(8,128)(4,1)S(1)} %fusion.115, bf16[4,192,8,128]{3,1,2,0:T(8,128)(2,1)} %get-tuple-element.288, s32[]{:T(128)} %get-tuple-element.274, bf16[4,1536,128]{2,1,0:T(8,128)(2,1)} %get-tuple-element.287), kind=kOutput, calls=%fused_computation.117.clone.1 | convolution fusion | flops 613418496 | bytes 10525696 | tf_op jit(solution)/shard_map/while/body/eval_jaxpr/sub | solution.py:82
  221.0 8.8 %bitcast_dynamic-update-slice_fusion.2 = f32[4,8,192,1536]{3,2,1,0:T(8,128)} fusion(f32[4,8,192,1536]{3,2,1,0:T(8,128)} %get-tuple-element.275, s32[]{:T(128)} %get-tuple-element.274, f32[8,192,1536]{2,1,0:T(8,128)} %get-tuple-element.262, f32[8,192]{1,0:T(8,128)S(1)} %get-tuple-element.263), kind=kLoop, calls=%fused_computation.39.clone.1 | loop fusion | flops 2359296 | bytes 18881024 | tf_op jit(solution)/shard_map/while/body/jit(dynamic_update_index_in_dim)/dynamic_update_slice | solution.py:91
  229.8 2.6 fusion.117
  232.4 20.9 %convert_element_type.42 = bf16[4,8,192,1536]{3,2,1,0:T(8,128)(2,1)} convert(f32[4,8,192,1536]{3,2,1,0:T(8,128)} %get-tuple-element.297) | non-fusion elementwise | flops 9437184 | bytes 56623104 | tf_op jit(solution)/shard_map/convert_element_type | solution.py:108
  254.8 52.5 %while.25 = (s32[]{:T(128)}, bf16[4,8,192,1536]{3,1,0,2:T(8,128)(2,1)}, bf16[4,192,8,128]{3,1,2,0:T(8,128)(2,1)}, f32[4,8,192,1536]{3,2,1,0:T(8,128)}, bf16[4,15...) while((s32[]{:T(128)}, ...), condition=%wide.region_14.15_spmd, body=%wide.region_12.14_spmd.sunk | while | flops 1216215552 | bytes 30688352 | solution.py:105
  255.2 4.8 fusion.109
  259.9 3.1 fusion.110
  263.1 4.8 copy_dynamic-update-slice_fusion.2
  268.2 4.8 fusion.109
  273.0 3.1 fusion.110
  276.1 4.7 copy_dynamic-update-slice_fusion.2
  281.2 4.8 fusion.109
  286.0 3.1 fusion.110
  289.2 4.9 copy_dynamic-update-slice_fusion.2
  294.4 4.8 fusion.109
  299.2 3.1 fusion.110
  302.3 5.0 %copy_dynamic-update-slice_fusion.2 = bf16[4,8,192,1536]{3,1,0,2:T(8,128)(2,1)} fusion(bf16[4,8,192,1536]{3,1,0,2:T(8,128)(2,1)} %get-tuple-element.304, s32[]{:T(128)} %get-tuple-element.303, bf16[1,8,192,1536]{3,2,1,0:T(8,128)(2,1)S(1)} %bitcast.197), kind=kLoop, calls=%fused_computation.23.clone.1 | loop fusion | bytes 9437696 | tf_op jit(solution)/shard_map/while/body/jit(dynamic_update_index_in_dim)/dynamic_update_slice | solution.py:105
  307.3 10.1 %fusion.65 = f32[4,128,1536]{2,1,0:T(8,128)} fusion(bf16[192,4,8,128]{3,2,1,0:T(8,128)(2,1)} %bitcast.68, bf16[4,8,192,1536]{3,1,0,2:T(8,128)(2,1)} %get-tuple-element.88), kind=kOutput, calls=%fused_computation.75 | convolution fusion | flops 2416705536 | bytes 23592960 | tf_op jit(solution)/shard_map/grqk,qgrd->kgd/dot_general | solution.py:111
  317.4 3.7 copy.42
  321.1 21.0 %fusion.63 = f32[4,128,1536,1]{2,1,0,3:T(8,128)} fusion(bf16[192,4,8,128]{3,2,1,0:T(8,128)(2,1)S(1)} %bitcast.213, bf16[4,8,192,1536]{3,2,1,0:T(8,128)(2,1)} %convert_element_type.42), kind=kOutput, calls=%fused_computation.71 | convolution fusion | flops 2415919104 | bytes 23592960 | tf_op jit(solution)/shard_map/grqk,qgrd->kgd/dot_general | solution.py:113
  342.1 3.7 copy.43
  345.8 6.5 %pad_maximum_fusion = f32[1536,1024]{1,0:T(8,128)} fusion(f32[1536,512]{1,0:T(8,128)} %copy.43, f32[1536,512]{1,0:T(8,128)} %copy.42), kind=kLoop, calls=%fused_computation.73 | loop fusion | flops 1572864 | bytes 12582912 | tf_op jit(solution)/shard_map/concatenate | solution.py:115
  356.1 4.0 gather_fusion.11
  360.2 7.2 %all-to-all-start.6 = ((bf16[16,24,4096]{2,1,0:T(8,128)(2,1)}), bf16[16,24,4096]{2,1,0:T(8,128)(2,1)}, u32[]{:S(2)}, u32[]{:S(2)}) async-start(bf16[16,24,4096]{2,1,0:T(8,128)(2,1)} %bitcast.207), calls=%async_computation.6 | async-start | bytes 6291456 | tf_op jit(solution)/shard_map/all_to_all | solution.py:130
  369.1 4.0 gather_fusion.7
  373.1 30.7 %all-to-all-done.6 = bf16[16,24,4096]{2,1,0:T(8,128)(2,1)} async-done(((bf16[16,24,4096]{2,1,0:T(8,128)(2,1)}), bf16[16,24,4096]{2,1,0:T(8,128)(2,1)}, u32[]{:S(2)}, u32[]{:S(2)}) %all-to-all-start.6) | async-done | bytes 3145760 | tf_op jit(solution)/shard_map/all_to_all | solution.py:130
  403.8 7.5 %all-to-all-start.4 = ((bf16[16,24,4096]{2,1,0:T(8,128)(2,1)}), bf16[16,24,4096]{2,1,0:T(8,128)(2,1)S(1)}, u32[]{:S(2)}, u32[]{:S(2)}) async-start(bf16[16,24,4096]{2,1,0:T(8,128)(2,1)} %bitcast.206), calls=%async_computation.4 | async-start | bytes 6291456 | tf_op jit(solution)/shard_map/all_to_all | solution.py:129
  415.1 34.7 %all-to-all-done.4 = bf16[16,24,4096]{2,1,0:T(8,128)(2,1)S(1)} async-done(((bf16[16,24,4096]{2,1,0:T(8,128)(2,1)}), bf16[16,24,4096]{2,1,0:T(8,128)(2,1)S(1)}, u32[]{:S(2)}, u32[]{:S(2)}) %all-to-all-start.4) | async-done | bytes 3145760 | tf_op jit(solution)/shard_map/all_to_all | solution.py:129
  449.8 7.0 %all-to-all-start.8 = ((bf16[16,24,512]{2,1,0:T(8,128)(2,1)}), bf16[16,24,512]{2,1,0:T(8,128)(2,1)}, u32[]{:S(2)}, u32[]{:S(2)}) async-start(bf16[16,24,512]{2,1,0:T(8,128)(2,1)} %bitcast.221), calls=%async_computation.9 | async-start | bytes 786432 | tf_op jit(solution)/shard_map/all_to_all | solution.py:132
  459.4 4.7 all-to-all-done.8
  464.1 6.0 %all-to-all-start.7 = ((bf16[16,24,512]{2,1,0:T(8,128)(2,1)}), bf16[16,24,512]{2,1,0:T(8,128)(2,1)S(1)}, u32[]{:S(2)}, u32[]{:S(2)}) async-start(bf16[16,24,512]{2,1,0:T(8,128)(2,1)} %bitcast.220), calls=%async_computation.8 | async-start | bytes 786432 | tf_op jit(solution)/shard_map/all_to_all | solution.py:131
  470.1 6.5 %gather_fusion.12 = bf16[192,4096]{1,0:T(8,128)(2,1)} fusion(bf16[384,4096]{1,0:T(8,128)(2,1)} %bitcast.31, s32[1024]{0:T(1024)S(1)} %pad_clamp_fusion), kind=kCustom, calls=%fused_computation.12 | custom fusion | bytes 3146496 | tf_op jit(solution)/shard_map/gather | solution.py:56
  476.6 2.7 gather_fusion.8
  479.3 2.8 gather_fusion.16
  (96 shorter events, 39.3 us)
Async XLA Ops:
  7.2 96.6 %copy-start = (s32[16,2]{0,1:T(2,128)S(1)}, s32[16,2]{0,1:T(2,128)}, u32[]{:S(2)}) copy-start(s32[16,2]{0,1:T(2,128)} %param.15) | copy-start | bytes 388
  8.8 1.2 copy-start.7
  10.1 21.8 %copy-start.5 = (bf16[192,512]{1,0:T(8,128)(2,1)S(1)}, bf16[192,512]{1,0:T(8,128)(2,1)}, u32[]{:S(2)}) copy-start(bf16[192,512]{1,0:T(8,128)(2,1)} %param.11) | copy-start | bytes 589828
  13.7 12.5 %all-to-all-start.1 = ((s32[16,1,24]{2,1,0:T(1,128)}), s32[16,1,24]{2,1,0:T(1,128)S(1)}, u32[]{:S(2)}, u32[]{:S(2)}) async-start(s32[16,1,24]{2,1,0:T(1,128)} %all_to_all.31), calls=%async_computation.1 | async-start | bytes 16384 | tf_op jit(solution)/shard_map/all_to_all | solution.py:34
  26.2 12.9 %all-to-all-start.3 = ((bf16[16,24,512]{2,1,0:T(8,128)(2,1)}), bf16[16,24,512]{2,1,0:T(8,128)(2,1)S(1)}, u32[]{:S(2)}, u32[]{:S(2)}) async-start(bf16[16,24,512]{2,1,0:T(8,128)(2,1)} %bitcast.19), calls=%async_computation.3 | async-start | bytes 786432 | tf_op jit(solution)/shard_map/all_to_all | solution.py:38
  39.1 12.9 %all-to-all-start = ((bf16[16,24,512]{2,1,0:T(8,128)(2,1)}), bf16[16,24,512]{2,1,0:T(8,128)(2,1)S(1)}, u32[]{:S(2)}, u32[]{:S(2)}) async-start(bf16[16,24,512]{2,1,0:T(8,128)(2,1)} %bitcast.13), calls=%async_computation | async-start | bytes 786432 | tf_op jit(solution)/shard_map/all_to_all | solution.py:37
  52.0 43.4 %all-to-all-start.2 = ((bf16[16,24,4096]{2,1,0:T(8,128)(2,1)}), bf16[16,24,4096]{2,1,0:T(8,128)(2,1)}, u32[]{:S(2)}, u32[]{:S(2)}) async-start(bf16[16,24,4096]{2,1,0:T(8,128)(2,1)} %bitcast.205), calls=%async_computation.2 | async-start | bytes 6291456 | tf_op jit(solution)/shard_map/all_to_all | solution.py:36
  58.2 88.2 %all-gather.7.cloned.1.call-start = ((), (), s32[]{:S(2)}) async-start(), calls=%async_computation.12 | async-start | bytes 1769472 | tf_op jit(solution)/shard_map/all_gather | solution.py:70
  95.4 44.8 %all-to-all-start.5 = ((bf16[16,24,4096]{2,1,0:T(8,128)(2,1)}), bf16[16,24,4096]{2,1,0:T(8,128)(2,1)S(1)}, u32[]{:S(2)}, u32[]{:S(2)}) async-start(bf16[16,24,4096]{2,1,0:T(8,128)(2,1)} %bitcast.204), calls=%async_computation.5 | async-start | bytes 6291456 | tf_op jit(solution)/shard_map/all_to_all | solution.py:39
  101.7 47.6 %all-gather.5.cloned.1.call-start = ((), (), s32[]{:S(2)}) async-start(), calls=%async_computation.11 | async-start | bytes 1769472 | tf_op jit(solution)/shard_map/all_gather | solution.py:69
  103.5 307.8 %reduce-scatter.2.cloned.1.call-start = ((), (), s32[]{:S(2)}) async-start(), calls=%async_computation.10 | async-start | bytes 7077888 | tf_op jit(solution)/shard_map/reduce_scatter | solution.py:114
  144.6 1.2 copy-start.3
  161.2 8.8 %copy-start.2 = (f32[8,192,1536]{2,1,0:T(8,128)S(1)}, f32[8,192,1536]{2,1,0:T(8,128)}, u32[]{:S(2)}) copy-start(f32[8,192,1536]{2,1,0:T(8,128)} %get-tuple-element.262) | copy-start | bytes 28311556 | tf_op jit(solution)/shard_map/while
  181.1 8.8 %copy-start.2 = (f32[8,192,1536]{2,1,0:T(8,128)S(1)}, f32[8,192,1536]{2,1,0:T(8,128)}, u32[]{:S(2)}) copy-start(f32[8,192,1536]{2,1,0:T(8,128)} %get-tuple-element.262) | copy-start | bytes 28311556 | tf_op jit(solution)/shard_map/while
  201.0 8.9 %copy-start.2 = (f32[8,192,1536]{2,1,0:T(8,128)S(1)}, f32[8,192,1536]{2,1,0:T(8,128)}, u32[]{:S(2)}) copy-start(f32[8,192,1536]{2,1,0:T(8,128)} %get-tuple-element.262) | copy-start | bytes 28311556 | tf_op jit(solution)/shard_map/while
  221.0 8.8 %copy-start.2 = (f32[8,192,1536]{2,1,0:T(8,128)S(1)}, f32[8,192,1536]{2,1,0:T(8,128)}, u32[]{:S(2)}) copy-start(f32[8,192,1536]{2,1,0:T(8,128)} %get-tuple-element.262) | copy-start | bytes 28311556 | tf_op jit(solution)/shard_map/while
  317.4 3.7 copy-start.4
  352.3 0.7 copy-start.6
  360.2 43.6 %all-to-all-start.6 = ((bf16[16,24,4096]{2,1,0:T(8,128)(2,1)}), bf16[16,24,4096]{2,1,0:T(8,128)(2,1)}, u32[]{:S(2)}, u32[]{:S(2)}) async-start(bf16[16,24,4096]{2,1,0:T(8,128)(2,1)} %bitcast.207), calls=%async_computation.6 | async-start | bytes 6291456 | tf_op jit(solution)/shard_map/all_to_all | solution.py:130
  403.8 46.0 %all-to-all-start.4 = ((bf16[16,24,4096]{2,1,0:T(8,128)(2,1)}), bf16[16,24,4096]{2,1,0:T(8,128)(2,1)S(1)}, u32[]{:S(2)}, u32[]{:S(2)}) async-start(bf16[16,24,4096]{2,1,0:T(8,128)(2,1)} %bitcast.206), calls=%async_computation.4 | async-start | bytes 6291456 | tf_op jit(solution)/shard_map/all_to_all | solution.py:129
  415.1 55.0 %copy-start.8 = (s32[192]{0:T(256)S(1)}, s32[192]{0:T(256)}, u32[]{:S(2)}) copy-start(s32[192]{0:T(256)} %copy-done.7) | copy-start | bytes 2308
  449.8 14.3 %all-to-all-start.8 = ((bf16[16,24,512]{2,1,0:T(8,128)(2,1)}), bf16[16,24,512]{2,1,0:T(8,128)(2,1)}, u32[]{:S(2)}, u32[]{:S(2)}) async-start(bf16[16,24,512]{2,1,0:T(8,128)(2,1)} %bitcast.221), calls=%async_computation.9 | async-start | bytes 786432 | tf_op jit(solution)/shard_map/all_to_all | solution.py:132
  464.1 17.9 %all-to-all-start.7 = ((bf16[16,24,512]{2,1,0:T(8,128)(2,1)}), bf16[16,24,512]{2,1,0:T(8,128)(2,1)S(1)}, u32[]{:S(2)}, u32[]{:S(2)}) async-start(bf16[16,24,512]{2,1,0:T(8,128)(2,1)} %bitcast.220), calls=%async_computation.8 | async-start | bytes 786432 | tf_op jit(solution)/shard_map/all_to_all | solution.py:131
  476.6 7.1 %copy-start.1 = (s32[16,2]{0,1:T(2,128)S(1)}, s32[16,2]{0,1:T(2,128)}, u32[]{:S(2)}) copy-start(s32[16,2]{0,1:T(2,128)} %param.15) | copy-start | bytes 388
Sparse Core Ops, SparseCore 0:
  64.9 26.8 all-gather.6
  104.8 26.8 all-gather.4
  352.4 45.4 reduce-scatter.1
where the time goes:
time: 499 us; the launch traced here: 490 us
  waiting for transfers between devices  126 us (25%)
  local copies, waits for them, and re-layouts  115 us (23%)
  matrix products  105 us (21%)
  other arithmetic  70.2 us (14%)
  starting transfers between devices  59.3 us (12%)
  between operations  14.3 us (3%)
    dynamic_update_slice x4, other arithmetic, local(): prob_all, att_all = lax.map(forward_group, (q_groups, k_groups, v_groups))  35.2 us
    all_to_all x1, waiting for transfers between devices, local(): lax.all_to_all(to_owners(attended_rows), 'dp', split_axis=0, concat_axis=...  34.7 us
    sub x4, matrix products, forward_group(): expo = jnp.exp(masked - top)  32 us
    all_to_all x1, waiting for transfers between devices, local(): lax.all_to_all(to_owners(grad_q), 'dp', split_axis=0, concat_axis=0, tile...  30.7 us
    all_to_all x1, waiting for transfers between devices, local(): lax.all_to_all(to_slots(queries), 'dp', split_axis=0, concat_axis=0, tile...  24.9 us
    all_to_all x1, waiting for transfers between devices, local(): lax.all_to_all(to_slots(grad_out), 'dp', split_axis=0, concat_axis=0, til...  23.4 us
    dot_general x1, matrix products, local(): jnp.einsum('grqk,qgrd->kgd', prob_b, d_heads, preferred_element_type=jnp....  21 us
    convert_element_type x1, other arithmetic, local(): prob_b = prob_all.astype(jnp.bfloat16)  20.9 us
  transfers between devices with their start and end apart: 12, of which 8 were waited for; matrix products, arithmetic and copies ran while one was open for 16% of the time, Pallas kernels for 0%

commit v1 on v0

v1 whole, which is shorter than its diff:
```python
import functools
import math

import jax
import jax.numpy as jnp
from jax import lax
from jax.experimental import pallas as pl
from jax.experimental.pallas import tpu as pltpu
from jax.sharding import PartitionSpec as P

D = 128
TOK = 192
CAP = 24
F32 = jnp.float32
BF16 = jnp.bfloat16
MESH = pl.DeviceIdType.MESH
VMEM = pl.BlockSpec(memory_space=pltpu.VMEM)
SMEM = pl.BlockSpec(memory_space=pltpu.SMEM)
ANY = pl.BlockSpec(memory_space=pl.ANY)
DMA = pltpu.SemaphoreType.DMA
NN = (((1,), (0,)), ((), ()))
NT = (((1,), (1,)), ((), ()))
TN = (((0,), (0,)), ((), ()))
TILE = 256
SCALE = 1.0 / math.sqrt(D)
EXP2 = SCALE * math.log2(math.e)


def dot(a, b, dims=NN):
    return lax.dot_general(a, b, dims, preferred_element_type=F32)


def iota(shape, axis):
    return lax.broadcasted_iota(jnp.int32, shape, axis)


def group_of(dest):
    return ((dest >> 9) * 43) >> 7


def place_of(dest):
    return dest - 192 * (((dest >> 6) * 171) >> 9)


NEAR = [(dx, dy) for dx in (-1, 0, 1) for dy in (-1, 0, 1) if (dx, dy) != (0, 0)]
FAR = [(2, 0), (2, 1), (2, -1), (0, 2), (1, 2), (-1, 2), (2, 2)]


class Here:
    def __init__(self):
        self.dp = lax.axis_index("dp")
        self.ctx = lax.axis_index("ctx")
        self.x, self.y = self.dp // 4, self.dp % 4

    def at(self, dx, dy):
        return ((self.x + (dx + 4)) % 4) * 4 + (self.y + (dy + 4)) % 4

    def peer(self, step):
        return (self.ctx + (step + 8)) % 8

    def partner(self):
        return self.ctx + 1 - 2 * (self.ctx % 2)


def greet(here, plane=False, column=False, partner=False):
    barrier = pltpu.get_barrier_semaphore()
    who = []
    if plane:
        who += [(here.at(*step), here.ctx) for step in NEAR]
    if column:
        who += [(here.dp, here.peer(step)) for step in range(1, 8)]
    if partner:
        who += [(here.dp, here.partner())]
    for device in who:
        pl.semaphore_signal(barrier, inc=1, device_id=device, device_id_type=MESH)
    pl.semaphore_wait(barrier, len(who))


class Plane:
    SCRATCH = 7

    @staticmethod
    def scratch(rows, cols):
        return [pltpu.VMEM((14, rows // 2, cols), BF16), DMA((8,)), DMA((8,)), DMA((14,)), DMA((14,)), DMA((14,)), DMA((14,)), DMA]

    def __init__(self, here, send, recv, scratch):
        relay, near_s, near_r, first_s, first_r, last_s, last_r, own = scratch
        half = send.shape[1] // 2
        me = here.dp
        self.near, self.near_in, self.first, self.first_in, self.last, self.last_in = [], [], [], [], [], []
        self.own = pltpu.make_async_copy(send.at[me], recv.at[me], own)

        def remote(src, dst, s, r, device):
            return pltpu.make_async_remote_copy(
                src_ref=src, dst_ref=dst, send_sem=s, recv_sem=r, device_id=(device, here.ctx), device_id_type=MESH
            )

        for i, (dx, dy) in enumerate(NEAR):
            to, source = here.at(dx, dy), here.at(-dx, -dy)
            self.near.append(remote(send.at[to], recv.at[me], near_s.at[i], near_r.at[i], to))
            self.near_in.append(remote(recv.at[source], recv.at[source], near_s.at[i], near_r.at[i], to))
        for i, (dx, dy) in enumerate(FAR):
            for e in range(2):
                sign, n = 1 - 2 * e, 2 * i + e
                rows = pl.ds(e * half, half)
                one = (sign if dx == 2 else dx, sign if dy == 2 else dy)
                two = (sign if dx == 2 else 0, sign if dy == 2 else 0)
                via, final = here.at(*one), here.at(*two)
                origin, source = here.at(-one[0], -one[1]), here.at(-dx, -dy)
                slot = relay.at[n]
                self.first.append(remote(send.at[here.at(dx, dy), rows], slot, first_s.at[n], first_r.at[n], via))
                self.first_in.append(remote(slot, slot, first_s.at[n], first_r.at[n], via))
                self.last.append(remote(slot, recv.at[origin, rows], last_s.at[n], last_r.at[n], final))
                landing = recv.at[source, rows]
                self.last_in.append(remote(landing, landing, last_s.at[n], last_r.at[n], final))

    def start(self):
        for c in self.first + self.near:
            c.start()
        self.own.start()

    def forward(self):
        for arrived, c in zip(self.first_in, self.last):
            arrived.wait_recv()
            c.start()

    def finish_in(self):
        for c in self.near_in + self.last_in:
            c.wait_recv()
        self.own.wait()

    def finish_out(self):
        for c in self.near + self.first + self.last:
            c.wait_send()


class Column:
    @staticmethod
    def scratch():
        return [DMA((8,)), DMA((8,)), DMA]

    def __init__(self, here, source, target, scratch):
        send_s, recv_s, own = scratch
        self.out, self.into = [], []
        self.own = pltpu.make_async_copy(source(here.ctx), target(here.ctx), own)
        for i in range(1, 8):
            to, origin = here.peer(i), here.peer(-i)

            def remote(src, dst):
                return pltpu.make_async_remote_copy(
                    src_ref=src, dst_ref=dst, send_sem=send_s.at[i], recv_sem=recv_s.at[i],
                    device_id=(here.dp, to), device_id_type=MESH,
                )

            self.out.append(remote(source(to), target(here.ctx)))
            self.into.append(remote(target(origin), target(origin)))

    def start(self):
        for c in self.out:
            c.start()
        self.own.start()

    def finish_in(self):
        for c in self.into:
            c.wait_recv()
        self.own.wait()

    def finish_out(self):
        for c in self.out:
            c.wait_send()


def cols(start, width):
    return pl.ds(pl.multiple_of(start, 128), width)


def hot_of(place_ref, pair):
    return jnp.where(place_ref[pair : pair + 1] == (iota((384, 768), 0) + 1).astype(F32), 1.0, 0.0).astype(BF16)


def pack_pair(hots, z_ref, pair, out_ref):
    width = z_ref.shape[2]
    x = dot(hots[2 * pair], z_ref[2 * pair]) + dot(hots[2 * pair + 1], z_ref[2 * pair + 1])
    out_ref[:, 48 * pair : 48 * pair + 48] = x.astype(BF16).reshape(16, 48, width)


def in_kernel(row_ref, col_ref, k_ref, v_ref, q_ref, d_ref,
              slots_ref, place_ref, kv_ref, kt_ref, vt_ref, gq0_ref, gq1_ref, pd_ref,
              info, infos, kvs, zkv, zq0, zq1, zd, hots, skv, rkv, sq0, sq1, swap_s, swap_r, *sems):
    here = Here()
    parity = here.ctx % 2
    dest_r, dest_c = row_ref[...], col_ref[...]
    g_r, g_c = group_of(dest_r), group_of(dest_c)
    same = (g_r == g_c) & (iota((TOK, TOK), 0) < iota((TOK, TOK), 1))
    rank = jnp.sum(jnp.where(same, 1.0, 0.0), axis=0, keepdims=True).astype(jnp.int32) + CAP * parity
    which = iota((8, TOK), 0)
    info[...] = jnp.where(
        which == 0, g_r * 48 + rank, jnp.where(which == 1, place_of(dest_r) + 1, jnp.where(which == 2, g_r, rank))
    )
    for z in range(4):
        kvs[:, 2 * z * D : 2 * z * D + D] = k_ref[:, z * D : z * D + D]
        kvs[:, 2 * z * D + D : 2 * z * D + 2 * D] = v_ref[:, z * D : z * D + D]

    cs = [sems[3 * i : 3 * i + 3] for i in range(5)]
    ps = [sems[15 + 8 * i : 23 + 8 * i] for i in range(3)]
    a_info = Column(here, lambda p: info, lambda p: infos.at[p], cs[0])
    a_kv = Column(here, lambda p: kvs.at[:, cols(p * D, D)], lambda p: zkv.at[p], cs[1])
    a_q0 = Column(here, lambda p: q_ref.at[:, cols(p * 512, 256)], lambda p: zq0.at[p], cs[2])
    a_q1 = Column(here, lambda p: q_ref.at[:, cols(p * 512 + 256, 256)], lambda p: zq1.at[p], cs[3])
    a_d = Column(here, lambda p: d_ref.at[:, cols(p * 512, 512)], lambda p: zd.at[p], cs[4])
    b_kv = Plane(here, skv, rkv, ps[0])
    b_q0 = Plane(here, sq0, gq0_ref, ps[1])
    b_q1 = Plane(here, sq1, gq1_ref, ps[2])

    greet(here, plane=True, column=True)
    a_info.start()
    a_kv.start()
    a_q0.start()
    a_q1.start()
    a_info.finish_in()
    which = iota((16, 32, D), 1)
    tail = jnp.zeros((16, 32, D), F32)
    for pair in range(4):
        laid = jnp.zeros((16, D), F32)
        for c in (2 * pair, 2 * pair + 1):
            hots[c] = jnp.where(iota((768, TOK), 0) == infos[c, 0:1], 1.0, 0.0).astype(BF16)
            slots_ref[c : c + 1] = infos[c, 0:1].astype(F32)
            named = jnp.where(iota((16, TOK), 0) == infos[c, 2:3], infos[c, 1:2].astype(F32), 0.0).astype(BF16)
            laned = jnp.where(iota((D, TOK), 0) == infos[c, 3:4], 1.0, 0.0).astype(BF16)
            laid += dot(named, laned, NT)
        tail = jnp.where(which == pair, laid.reshape(16, 1, D), tail)
    a_kv.finish_in()
    for pair in range(4):
        pack_pair(hots, zkv, pair, skv)
    skv[:, TOK:] = tail.astype(BF16)
    b_kv.start()
    a_q0.finish_in()
    for pair in range(4):
        pack_pair(hots, zq0, pair, sq0)
    b_q0.start()
    b_kv.forward()
    a_q1.finish_in()
    a_d.start()
    for pair in range(4):
        pack_pair(hots, zq1, pair, sq1)
    b_q1.start()
    b_q0.forward()

    b_kv.finish_in()
    total = jnp.zeros((8, 768), F32)
    for s in range(16):
        mine = jnp.concatenate([rkv[s, TOK : TOK + 16].astype(F32)[:8], jnp.zeros((8, 640), F32)], axis=1)
        total += mine if s == 0 else pltpu.roll(mine, 48 * s, 1)
    odd = (iota((8, 768), 1) % 48) >= CAP
    place_ref[...] = jnp.where(odd & (total > 0.0), total + 192.0, total)
    for pair in range(4):
        x = rkv[:, 48 * pair : 48 * pair + 48].reshape(768, D)
        kv_ref[parity, 384 * pair : 384 * pair + 384] = dot(hot_of(place_ref, pair), x).astype(BF16)
    swap = pltpu.make_async_remote_copy(
        src_ref=kv_ref.at[parity], dst_ref=kv_ref.at[parity], send_sem=swap_s, recv_sem=swap_r,
        device_id=(here.dp, here.partner()), device_id_type=MESH,
    )
    swap.start()
    b_q1.forward()
    swapped = kv_ref.at[1 - parity]
    pltpu.make_async_remote_copy(
        src_ref=swapped, dst_ref=swapped, send_sem=swap_s, recv_sem=swap_r,
        device_id=(here.dp, here.partner()), device_id_type=MESH,
    ).wait_recv()
    kt_ref[...] = jnp.transpose(kv_ref[0].astype(F32)).astype(BF16)
    vt_ref[...] = jnp.transpose(kv_ref[1].astype(F32)).astype(BF16)
    a_d.finish_in()
    for pair in range(4):
        pack_pair(hots, zd, pair, pd_ref)
    b_q0.finish_in()
    b_q1.finish_in()
    swap.wait_send()
    for c in (a_info, a_kv, a_q0, a_q1, a_d, b_kv, b_q0, b_q1):
        c.finish_out()


def bring_in(destination, keys, values, queries, grad_out):
    return pl.pallas_call(
        in_kernel,
        out_shape=(
            jax.ShapeDtypeStruct((8, TOK), F32),
            jax.ShapeDtypeStruct((8, 768), F32),
            jax.ShapeDtypeStruct((2, 1536, D), BF16),
            jax.ShapeDtypeStruct((D, 1536), BF16),
            jax.ShapeDtypeStruct((D, 1536), BF16),
            jax.ShapeDtypeStruct((16, TOK, 256), BF16),
            jax.ShapeDtypeStruct((16, TOK, 256), BF16),
            jax.ShapeDtypeStruct((16, TOK, 512), BF16),
        ),
        in_specs=[VMEM] * 4 + [ANY] * 2,
        out_specs=(VMEM,) * 5 + (ANY, ANY, VMEM),
        scratch_shapes=[
            pltpu.VMEM((8, TOK), jnp.int32),
            pltpu.VMEM((8, 8, TOK), jnp.int32),
            pltpu.VMEM((TOK, 1024), BF16),
            pltpu.VMEM((8, TOK, D), BF16),
            pltpu.VMEM((8, TOK, 256), BF16),
            pltpu.VMEM((8, TOK, 256), BF16),
            pltpu.VMEM((8, TOK, 512), BF16),
            pltpu.VMEM((8, 768, TOK), BF16),
            pltpu.VMEM((16, TOK + 32, D), BF16),
            pltpu.VMEM((16, TOK + 32, D), BF16),
            pltpu.VMEM((16, TOK, 256), BF16),
            pltpu.VMEM((16, TOK, 256), BF16),
            DMA,
            DMA,
        ]
        + Column.scratch() * 5
        + Plane.scratch(TOK + 32, D) + Plane.scratch(TOK, 256) + Plane.scratch(TOK, 256),
        compiler_params=pltpu.CompilerParams(collective_id=0, has_side_effects=True, vmem_limit_bytes=44 << 20),
        name="bring_in",
    )(destination.reshape(1, TOK), destination.reshape(TOK, 1), keys, values, queries, grad_out)


def tiles():
    for j in range(6):
        low = 0 if j < 4 else 512
        yield j, list(range(low, (j + 1) * TILE, TILE))


def allowed(j, k, end):
    diagonal, mixed = k == j * TILE, j >= 2
    if not diagonal and not mixed:
        return None
    kp = k + iota((TILE, TILE), 0)
    qp = j * TILE + iota((1, TILE), 1)
    mask = None
    if mixed:
        mask = kp >= jnp.where(qp >= end, end, 0)
    if diagonal:
        causal = kp <= qp
        mask = causal if mask is None else mask & causal
    return mask


def forward_head(h, end, q_ref, k_ref, vt_ref, o_ref, lse_ref):
    for j, ks in tiles():
        rows = slice(j * TILE, j * TILE + TILE)
        q = q_ref[h, rows]
        scores = []
        for k in ks:
            s = dot(k_ref[0, k : k + TILE], q, NT)
            mask = allowed(j, k, end)
            scores.append(s if mask is None else jnp.where(mask, s, -jnp.inf))
        top = jnp.max(functools.reduce(jnp.maximum, scores), axis=0, keepdims=True)
        expo = [jnp.exp2((s - top) * EXP2) for s in scores]
        total = jnp.sum(functools.reduce(jnp.add, expo), axis=0, keepdims=True)
        inverse = 1.0 / total
        att = jnp.zeros((D, TILE), F32)
        for k, e in zip(ks, expo):
            att += dot(vt_ref[:, k : k + TILE], (e * inverse).astype(BF16))
        o_ref[h, rows] = jnp.transpose(att).astype(BF16)
        lse_ref[h, :, rows] = top * EXP2 + jnp.log2(total)


def forward_kernel(end_ref, place_ref, kv_ref, vt_ref, gq0_ref, gq1_ref, pd_ref,
                   q_ref, o_ref, lse_ref, po_ref, gd_ref, *sems):
    here = Here()
    b_d = Plane(here, pd_ref, gd_ref, sems)
    greet(here, plane=True)
    b_d.start()
    end = end_ref[0]
    for pair in range(4):
        hot = hot_of(place_ref, pair)
        for n, got in enumerate((gq0_ref, gq1_ref)):
            x = dot(hot, got[:, 48 * pair : 48 * pair + 48].reshape(768, 256)).astype(BF16)
            for h in range(2):
                q_ref[2 * n + h, 384 * pair : 384 * pair + 384] = x[:, h * D : h * D + D]

    @pl.loop(0, 2)
    def _(h):
        forward_head(h, end, q_ref, kv_ref, vt_ref, o_ref, lse_ref)

    b_d.forward()

    @pl.loop(2, 4)
    def _(h):
        forward_head(h, end, q_ref, kv_ref, vt_ref, o_ref, lse_ref)

    for pair in range(4):
        x = jnp.concatenate([o_ref[h, 384 * pair : 384 * pair + 384] for h in range(4)], axis=1)
        po_ref[:, 48 * pair : 48 * pair + 48] = dot(hot_of(place_ref, pair), x, TN).astype(BF16).reshape(16, 48, 512)
    b_d.finish_in()
    b_d.finish_out()


def forward(end, place, kv, vt, gq0, gq1, pd):
    return pl.pallas_call(
        forward_kernel,
        out_shape=(
            jax.ShapeDtypeStruct((4, 1536, D), BF16),
            jax.ShapeDtypeStruct((4, 1536, D), BF16),
            jax.ShapeDtypeStruct((4, 1, 1536), F32),
            jax.ShapeDtypeStruct((16, TOK, 512), BF16),
            jax.ShapeDtypeStruct((16, TOK, 512), BF16),
        ),
        in_specs=[SMEM] + [VMEM] * 5 + [ANY],
        out_specs=(VMEM,) * 4 + (ANY,),
        scratch_shapes=Plane.scratch(TOK, 512),
        compiler_params=pltpu.CompilerParams(collective_id=1, has_side_effects=True, vmem_limit_bytes=44 << 20),
        name="forward",
    )(end, place, kv, vt, gq0, gq1, pd)


def backward_head(h, end, q_ref, d_ref, o_ref, lse_ref, kv_ref, kt_ref, g_ref, gq_ref):
    for j, ks in tiles():
        rows = slice(j * TILE, j * TILE + TILE)
        q, d = q_ref[h, rows], d_ref[h, rows]
        product = d.astype(F32) * o_ref[h, rows].astype(F32)
        delta = jnp.sum(jnp.transpose(product), axis=0, keepdims=True)
        lse = lse_ref[h, :, rows]
        gq = jnp.zeros((D, TILE), F32)
        for k in ks:
            keys = slice(k, k + TILE)
            p = jnp.exp2(dot(kv_ref[0, keys], q, NT) * EXP2 - lse)
            mask = allowed(j, k, end)
            if mask is not None:
                p = jnp.where(mask, p, 0.0)
            dp = dot(kv_ref[1, keys], d, NT)
            ds = (p * (dp - delta)).astype(BF16)
            g_ref[1, keys] += dot(p.astype(BF16), d)
            g_ref[0, keys] += dot(ds, q)
            gq += dot(kt_ref[:, keys], ds)
        gq_ref[h, rows] = jnp.transpose(gq * SCALE).astype(BF16)


def backward_kernel(end_ref, place_ref, kv_ref, kt_ref, gd_ref, q_ref, o_ref, lse_ref, po_ref,
                    pq_ref, pkv_ref, go_ref,
                    d_ref, gq_ref, g_ref, landed, swap_s, swap_r, *sems):
    here = Here()
    parity = here.ctx % 2
    b_o = Plane(here, po_ref, go_ref, sems)
    greet(here, plane=True, partner=True)
    b_o.start()
    end = end_ref[0]
    g_ref[...] = jnp.zeros_like(g_ref)
    for pair in range(4):
        x = dot(hot_of(place_ref, pair), gd_ref[:, 48 * pair : 48 * pair + 48].reshape(768, 512)).astype(BF16)
        for h in range(4):
            d_ref[h, 384 * pair : 384 * pair + 384] = x[:, h * D : h * D + D]

    @pl.loop(0, 2)
    def _(h):
        backward_head(h, end, q_ref, d_ref, o_ref, lse_ref, kv_ref, kt_ref, g_ref, gq_ref)

    b_o.forward()

    @pl.loop(2, 4)
    def _(h):
        backward_head(h, end, q_ref, d_ref, o_ref, lse_ref, kv_ref, kt_ref, g_ref, gq_ref)

    swap = pltpu.make_async_remote_copy(
        src_ref=g_ref.at[1 - parity], dst_ref=landed, send_sem=swap_s, recv_sem=swap_r,
        device_id=(here.dp, here.partner()), device_id_type=MESH,
    )
    swap.start()
    for pair in range(4):
        x = jnp.concatenate([gq_ref[h, 384 * pair : 384 * pair + 384] for h in range(4)], axis=1)
        pq_ref[:, 48 * pair : 48 * pair + 48] = dot(hot_of(place_ref, pair), x, TN).astype(BF16).reshape(16, 48, 512)
    swap.wait_recv()
    factor = jnp.where(parity == 0, SCALE, 1.0).astype(F32)
    for pair in range(4):
        rows = slice(384 * pair, 384 * pair + 384)
        x = ((g_ref[parity, rows] + landed[rows]) * factor).astype(BF16)
        pkv_ref[:, 48 * pair : 48 * pair + 48] = dot(hot_of(place_ref, pair), x, TN).astype(BF16).reshape(16, 48, D)
    b_o.finish_in()
    swap.wait_send()
    b_o.finish_out()


def backward(end, place, kv, kt, gd, q, o, lse, po):
    return pl.pallas_call(
        backward_kernel,
        out_shape=(
            jax.ShapeDtypeStruct((16, TOK, 512), BF16),
            jax.ShapeDtypeStruct((16, TOK, D), BF16),
            jax.ShapeDtypeStruct((16, TOK, 512), BF16),
        ),
        in_specs=[SMEM] + [VMEM] * 7 + [ANY],
        out_specs=(VMEM, VMEM, ANY),
        scratch_shapes=[
            pltpu.VMEM((4, 1536, D), BF16),
            pltpu.VMEM((4, 1536, D), BF16),
            pltpu.VMEM((2, 1536, D), F32),
            pltpu.VMEM((1536, D), F32),
            DMA,
            DMA,
        ]
        + Plane.scratch(TOK, 512),
        compiler_params=pltpu.CompilerParams(collective_id=2, has_side_effects=True, vmem_limit_bytes=44 << 20),
        name="backward",
    )(end, place, kv, kt, gd, q, o, lse, po)


def out_kernel(slots_ref, go_ref, pq_ref, pkv_ref, oo_ref, oq_ref, ok_ref, ov_ref,
               gq, gkv, zo, zq, zkv, okv, hots, *sems):
    here = Here()
    cs = [sems[3 * i : 3 * i + 3] for i in range(3)]
    ps = [sems[9 + 8 * i : 17 + 8 * i] for i in range(2)]
    b_q = Plane(here, pq_ref, gq, ps[0])
    b_kv = Plane(here, pkv_ref, gkv, ps[1])
    a_o = Column(here, lambda p: zo.at[p], lambda p: oo_ref.at[:, cols(p * 512, 512)], cs[0])
    a_q = Column(here, lambda p: zq.at[p], lambda p: oq_ref.at[:, cols(p * 512, 512)], cs[1])
    a_kv = Column(here, lambda p: zkv.at[p], lambda p: okv.at[:, cols(p * D, D)], cs[2])
    greet(here, plane=True, column=True)
    b_q.start()
    b_kv.start()
    slot_c = jnp.transpose(slots_ref[...])

    def unpack(got, z):
        for pair in range(4):
            x = got[:, 48 * pair : 48 * pair + 48].reshape(768, got.shape[2])
            for c in (2 * pair, 2 * pair + 1):
                z[c] = dot(hots[c], x).astype(BF16)

    for c in range(8):
        hots[c] = jnp.where(iota((TOK, 768), 1).astype(F32) == slot_c[:, c : c + 1], 1.0, 0.0).astype(BF16)
    unpack(go_ref, zo)
    a_o.start()
    b_q.forward()
    b_kv.forward()
    b_q.finish_in()
    unpack(gq, zq)
    a_q.start()
    b_kv.finish_in()
    unpack(gkv, zkv)
    a_kv.start()
    a_kv.finish_in()
    for z in range(4):
        ok_ref[:, z * D : z * D + D] = okv[:, 2 * z * D : 2 * z * D + D]
        ov_ref[:, z * D : z * D + D] = okv[:, 2 * z * D + D : 2 * z * D + 2 * D]
    a_o.finish_in()
    a_q.finish_in()
    for c in (b_q, b_kv, a_o, a_q, a_kv):
        c.finish_out()


def take_back(slots, go, pq, pkv):
    return pl.pallas_call(
        out_kernel,
        out_shape=(
            jax.ShapeDtypeStruct((TOK, 4096), BF16),
            jax.ShapeDtypeStruct((TOK, 4096), BF16),
            jax.ShapeDtypeStruct((TOK, 512), BF16),
            jax.ShapeDtypeStruct((TOK, 512), BF16),
        ),
        in_specs=[VMEM, VMEM, ANY, ANY],
        out_specs=(ANY, ANY, VMEM, VMEM),
        scratch_shapes=[
            pltpu.VMEM((16, TOK, 512), BF16),
            pltpu.VMEM((16, TOK, D), BF16),
            pltpu.VMEM((8, TOK, 512), BF16),
            pltpu.VMEM((8, TOK, 512), BF16),
            pltpu.VMEM((8, TOK, D), BF16),
            pltpu.VMEM((TOK, 1024), BF16),
            pltpu.VMEM((8, TOK, 768), BF16),
        ]
        + Column.scratch() * 3
        + Plane.scratch(TOK, 512) + Plane.scratch(TOK, D),
        compiler_params=pltpu.CompilerParams(collective_id=3, has_side_effects=True, vmem_limit_bytes=44 << 20),
        name="take_back",
    )(slots, go, pq, pkv)


def local(queries, keys, values, grad_out, destination, lengths):
    end = lax.dynamic_slice(lengths, (lax.axis_index("dp"), 0), (1, 1)).reshape(1)
    slots, place, kv, kt, vt, gq0, gq1, pd = bring_in(destination, keys, values, queries, grad_out)
    q, o, lse, po, gd = forward(end, place, kv, vt, gq0, gq1, pd)
    pq, pkv, go = backward(end, place, kv, kt, gd, q, o, lse, po)
    return take_back(slots, go, pq, pkv)


def solution(mesh):
    rows = P(("dp", "ctx"), None)
    return jax.shard_map(
        local,
        mesh=mesh,
        in_specs=(rows, rows, rows, rows, P(("dp", "ctx")), P()),
        out_specs=(rows, rows, rows, rows),
        check_vma=False,
    )
```

time: 499 us -> 267 us (0.54); the launches traced: 490 us -> 264 us
  Pallas kernels: 0 us -> 249 us
  waiting for transfers between devices: 126 us -> 0 us
  matrix products: 105 us -> 0 us
  local copies, waits for them, and re-layouts: 115 us -> 14.5 us
  other arithmetic: 70.2 us -> 0 us
  starting transfers between devices: 59.3 us -> 0 us
  between operations: 14.3 us -> 0.71 us
    pallas_call x0 -> x4, Pallas kernels: none -> 249 us  [the longest x1 80.3 us: take_back(): pl.pallas_call(out_kernel, out_shape=(jax.ShapeDtypeStruct((TOK, 4096), B...]
    all_to_all x9 -> x0, waiting for transfers between devices: 126 us -> none  [the longest x1 34.7 us: local(): lax.all_to_all(to_owners(attended_rows), 'dp', split_axis=0, concat_axis=...]
    dot_general x14 -> x0, matrix products: 73.3 us -> none  [the longest x1 21 us: local(): jnp.einsum('grqk,qgrd->kgd', prob_b, d_heads, preferred_element_type=jnp....]
    all_to_all x9 -> x0, starting transfers between devices: 59 us -> none  [the longest x1 7.49 us: local(): lax.all_to_all(to_owners(attended_rows), 'dp', split_axis=0, concat_axis=...]
    gather x17 -> x0, local copies, waits for them, and re-layouts: 55.4 us -> none  [the longest x4 13.6 us: read_back(): return returned.reshape(n_dp * cap, -1)[slot_of]]
    dynamic_update_slice x4 -> x0, other arithmetic: 35.2 us -> none  [local(): prob_all, att_all = lax.map(forward_group, (q_groups, k_groups, v_groups))]
    sub x4 -> x0, matrix products: 32 us -> none  [forward_group(): expo = jnp.exp(masked - top)]
    convert_element_type x1 -> x0, other arithmetic: 20.9 us -> none  [local(): prob_b = prob_all.astype(jnp.bfloat16)]
  transfers between devices with their start and end apart: 12 -> 0, of which waited for: 8 -> 0; matrix products, arithmetic and copies ran while one was open for 16% -> 0% of each run, Pallas kernels for 0% -> 0%
where the time goes in v1:
time: 267 us; the launch traced here: 264 us
  Pallas kernels  249 us (93%)
  local copies, waits for them, and re-layouts  14.5 us (5%)
    pallas_call x1, Pallas kernels, take_back(): pl.pallas_call(out_kernel, out_shape=(jax.ShapeDtypeStruct((TOK, 4096), B...  80.3 us
    pallas_call x1, Pallas kernels, bring_in(): pl.pallas_call(in_kernel, out_shape=(jax.ShapeDtypeStruct((8, TOK), F32),...  67.5 us
    pallas_call x1, Pallas kernels, backward(): pl.pallas_call(backward_kernel, out_shape=(jax.ShapeDtypeStruct((16, TOK,...  52.1 us
    pallas_call x1, Pallas kernels, forward(): pl.pallas_call(forward_kernel, out_shape=(jax.ShapeDtypeStruct((4, 1536,...  48.9 us
    unnamed x20, local copies, waits for them, and re-layouts  13.2 us

profile of v1, /device:TPU:16, one launch (start us, length us, event | category | flops | bytes accessed | tf_op | source)
XLA Modules:
  0.0 264.0 jit_solution(2744664251755954314)
XLA Ops:
  0.6 0.0 copy-start
  0.6 0.7 copy-done
  1.3 0.6 constant_dynamic-slice_fusion
  1.9 0.8 copy.10.col_ref
  2.7 0.0 copy-start.3
  2.7 1.4 copy-done.3
  4.1 0.0 copy-start.4
  4.1 1.4 copy-done.4
  5.5 0.0 copy-start.5
  5.5 0.9 copy-done.5
  6.4 0.0 copy-start.6
  6.4 0.9 copy-done.6
  7.4 0.0 copy-start.7
  7.4 0.7 copy-done.7
  8.0 67.5 %bring_in.1 = (f32[8,192]{1,0:T(8,128)S(1)}, f32[8,768]{1,0:T(8,128)S(1)}, bf16[2,1536,128]{2,1,0:T(8,128)(2,1)S(1)}, bf16[128,1536]{1,0:T(8,128)(2,1)S(1)}, bf1...) custom-call(s32[1,192]{1,0:T(1,128)S(1)} %bitcast.4, ...), custom_call_target="tpu_custom_call" | custom-call | tf_op jit(solution)/shard_map/bring_in/pallas_call | solution.py:283
  75.6 48.9 %forward.1 = (bf16[4,1536,128]{2,1,0:T(8,128)(2,1)S(1)}, bf16[4,1536,128]{2,1,0:T(8,128)(2,1)S(1)}, f32[4,1,1536]{2,1,0:T(1,128)S(1)}, bf16[16,192,512]{2,1,0:T(8,128)(2,1)}, bf16[16,192,512]{2,1,0:T(8,128)(2,1)}) custom-call(s32[1]{0:T(128)} %bitcast.2.end_ref, f32[8,768]{1,0:T(8,128)S(1)} %get-tuple-element.21.place_ref, ...), custom_call_target="tpu_custom_call" | custom-call | tf_op jit(solution)/shard_map/forward/pallas_call | solution.py:393
  124.5 52.1 %backward.1 = (bf16[16,192,512]{2,1,0:T(8,128)(2,1)S(1)}, bf16[16,192,128]{2,1,0:T(8,128)(2,1)S(1)}, bf16[16,192,512]{2,1,0:T(8,128)(2,1)}) custom-call(s32[1]{0:T(128)} %bitcast.2.end_ref, f32[8,768]{1,0:T(8,128)S(1)} %get-tuple-element.21.place_ref, bf16[2,1536,128]{2,1,0:T(8,128)(2,1)S(1)} %get-tuple-element.22.kv_ref, ...), custom_call_target="tpu_custom_call" | custom-call | tf_op jit(solution)/shard_map/backward/pallas_call | solution.py:477
  176.6 0.0 copy-start.1
  176.6 1.6 copy-done.1
  178.2 0.0 copy-start.2
  178.2 1.9 copy-done.2
  180.1 80.3 %take_back.1 = (bf16[192,4096]{1,0:T(8,128)(2,1)S(1)}, bf16[192,4096]{1,0:T(8,128)(2,1)S(1)}, bf16[192,512]{1,0:T(8,128)(2,1)S(1)}, bf16[192,512]{1,0:T(8,128)(2,1)S(1)}) custom-call(f32[8,192]{1,0:T(8,128)S(1)} %get-tuple-element.20.slots_ref, bf16[16,192,512]{2,1,0:T(8,128)(2,1)S(1)} %copy-done.2, bf16[16,192,512]{2,1,0:T(8,128)(2,1)} %copy-done.1, ...), custom_call_target="tpu_custom_call" | custom-call | tf_op jit(solution)/shard_map/take_back/pallas_call | solution.py:544
  260.4 1.1 copy.15
  261.5 1.1 copy.16
  262.7 0.7 copy.17
  263.4 0.7 copy.18
Async XLA Ops:
  0.6 0.7 copy-start
  2.7 1.4 copy-start.3
  4.1 1.4 copy-start.4
  5.5 0.9 copy-start.5
  6.4 0.9 copy-start.6
  7.4 0.7 copy-start.7
  176.6 1.6 copy-start.1
  178.2 1.9 copy-start.2

commit v2 on v1

--- a/solution.py
+++ b/solution.py
@@ -17,6 +17,7 @@
 VMEM = pl.BlockSpec(memory_space=pltpu.VMEM)
 SMEM = pl.BlockSpec(memory_space=pltpu.SMEM)
 ANY = pl.BlockSpec(memory_space=pl.ANY)
+HBM = pl.BlockSpec(memory_space=pltpu.HBM)
 DMA = pltpu.SemaphoreType.DMA
 NN = (((1,), (0,)), ((), ()))
 NT = (((1,), (1,)), ((), ()))
@@ -42,8 +43,8 @@
     return dest - 192 * (((dest >> 6) * 171) >> 9)
 
 
-NEAR = [(dx, dy) for dx in (-1, 0, 1) for dy in (-1, 0, 1) if (dx, dy) != (0, 0)]
-FAR = [(2, 0), (2, 1), (2, -1), (0, 2), (1, 2), (-1, 2), (2, 2)]
+STEPS = [(2, 2), (2, 1), (1, 2), (2, -1), (-1, 2), (1, 1), (-1, -1), (1, -1), (-1, 1), (2, 0), (0, 2),
+         (1, 0), (-1, 0), (0, 1), (0, -1)]
 
 
 class Here:
@@ -66,7 +67,7 @@
     barrier = pltpu.get_barrier_semaphore()
     who = []
     if plane:
-        who += [(here.at(*step), here.ctx) for step in NEAR]
+        who += [(here.at(*step), here.ctx) for step in STEPS]
     if column:
         who += [(here.dp, here.peer(step)) for step in range(1, 8)]
     if partner:
@@ -77,60 +78,42 @@
 
 
 class Plane:
-    SCRATCH = 7
+    COUNT = 3
 
     @staticmethod
-    def scratch(rows, cols):
-        return [pltpu.VMEM((14, rows // 2, cols), BF16), DMA((8,)), DMA((8,)), DMA((14,)), DMA((14,)), DMA((14,)), DMA((14,)), DMA]
-
-    def __init__(self, here, send, recv, scratch):
-        relay, near_s, near_r, first_s, first_r, last_s, last_r, own = scratch
-        half = send.shape[1] // 2
+    def scratch():
+        return [DMA((15,)), DMA((15,)), DMA]
+
+    def __init__(self, here, send, recv, scratch, order=tuple(range(15))):
+        send_s, recv_s, own = scratch
         me = here.dp
-        self.near, self.near_in, self.first, self.first_in, self.last, self.last_in = [], [], [], [], [], []
+        self.out, self.into = [], []
         self.own = pltpu.make_async_copy(send.at[me], recv.at[me], own)
-
-        def remote(src, dst, s, r, device):
-            return pltpu.make_async_remote_copy(
-                src_ref=src, dst_ref=dst, send_sem=s, recv_sem=r, device_id=(device, here.ctx), device_id_type=MESH
-            )
-
-        for i, (dx, dy) in enumerate(NEAR):
+        for i in order:
+            dx, dy = STEPS[i]
             to, source = here.at(dx, dy), here.at(-dx, -dy)
-            self.near.append(remote(send.at[to], recv.at[me], near_s.at[i], near_r.at[i], to))
-            self.near_in.append(remote(recv.at[source], recv.at[source], near_s.at[i], near_r.at[i], to))
-        for i, (dx, dy) in enumerate(FAR):
-            for e in range(2):
-                sign, n = 1 - 2 * e, 2 * i + e
-                rows = pl.ds(e * half, half)
-                one = (sign if dx == 2 else dx, sign if dy == 2 else dy)
-                two = (sign if dx == 2 else 0, sign if dy == 2 else 0)
-                via, final = here.at(*one), here.at(*two)
-                origin, source = here.at(-one[0], -one[1]), here.at(-dx, -dy)
-                slot = relay.at[n]
-                self.first.append(remote(send.at[here.at(dx, dy), rows], slot, first_s.at[n], first_r.at[n], via))
-                self.first_in.append(remote(slot, slot, first_s.at[n], first_r.at[n], via))
-                self.last.append(remote(slot, recv.at[origin, rows], last_s.at[n], last_r.at[n], final))
-                landing = recv.at[source, rows]
-                self.last_in.append(remote(landing, landing, last_s.at[n], last_r.at[n], final))
+
+            def remote(src, dst):
+                return pltpu.make_async_remote_copy(
+                    src_ref=src, dst_ref=dst, send_sem=send_s.at[i], recv_sem=recv_s.at[i],
+                    device_id=(to, here.ctx), device_id_type=MESH,
+                )
+
+            self.out.append(remote(send.at[to], recv.at[me]))
+            self.into.append(remote(recv.at[source], recv.at[source]))
 
     def start(self):
-        for c in self.first + self.near:
+        for c in self.out:
             c.start()
         self.own.start()
 
-    def forward(self):
-        for arrived, c in zip(self.first_in, self.last):
-            arrived.wait_recv()
-            c.start()
-
     def finish_in(self):
-        for c in self.near_in + self.last_in:
+        for c in self.into:
             c.wait_recv()
         self.own.wait()
 
     def finish_out(self):
-        for c in self.near + self.first + self.last:
+        for c in self.out:
             c.wait_send()
 
 
@@ -184,25 +167,31 @@
     out_ref[:, 48 * pair : 48 * pair + 48] = x.astype(BF16).reshape(16, 48, width)
 
 
-def in_kernel(row_ref, col_ref, k_ref, v_ref, q_ref, d_ref,
+def in_kernel(row_ref, k_ref, v_ref, q_ref, d_ref,
               slots_ref, place_ref, kv_ref, kt_ref, vt_ref, gq0_ref, gq1_ref, pd_ref,
-              info, infos, kvs, zkv, zq0, zq1, zd, hots, skv, rkv, sq0, sq1, swap_s, swap_r, *sems):
+              load, info, infos, kvs, zkv, zq0, zq1, zd, hots, skv, rkv, sq0, sq1, swap_s, swap_r, *sems):
     here = Here()
     parity = here.ctx % 2
-    dest_r, dest_c = row_ref[...], col_ref[...]
-    g_r, g_c = group_of(dest_r), group_of(dest_c)
-    same = (g_r == g_c) & (iota((TOK, TOK), 0) < iota((TOK, TOK), 1))
+    loads = []
+    for z in range(4):
+        for e, ref in enumerate((k_ref, v_ref)):
+            to = kvs.at[:, pl.ds((2 * z + e) * D, D)]
+            loads.append(pltpu.make_async_copy(ref.at[:, pl.ds(z * D, D)], to, load.at[2 * z + e]))
+    for c in loads:
+        c.start()
+    dest_r = row_ref[...]
+    g_r = group_of(dest_r)
+    g_c = jnp.transpose(jnp.broadcast_to(g_r.astype(F32), (8, TOK)))[:, 0:1]
+    same = (g_r.astype(F32) == g_c) & (iota((TOK, TOK), 0) < iota((TOK, TOK), 1))
     rank = jnp.sum(jnp.where(same, 1.0, 0.0), axis=0, keepdims=True).astype(jnp.int32) + CAP * parity
     which = iota((8, TOK), 0)
     info[...] = jnp.where(
         which == 0, g_r * 48 + rank, jnp.where(which == 1, place_of(dest_r) + 1, jnp.where(which == 2, g_r, rank))
     )
-    for z in range(4):
-        kvs[:, 2 * z * D : 2 * z * D + D] = k_ref[:, z * D : z * D + D]
-        kvs[:, 2 * z * D + D : 2 * z * D + 2 * D] = v_ref[:, z * D : z * D + D]
-
+    for c in loads:
+        c.wait()
     cs = [sems[3 * i : 3 * i + 3] for i in range(5)]
-    ps = [sems[15 + 8 * i : 23 + 8 * i] for i in range(3)]
+    ps = [sems[15 + 3 * i : 18 + 3 * i] for i in range(3)]
     a_info = Column(here, lambda p: info, lambda p: infos.at[p], cs[0])
     a_kv = Column(here, lambda p: kvs.at[:, cols(p * D, D)], lambda p: zkv.at[p], cs[1])
     a_q0 = Column(here, lambda p: q_ref.at[:, cols(p * 512, 256)], lambda p: zq0.at[p], cs[2])
@@ -238,13 +227,11 @@
     for pair in range(4):
         pack_pair(hots, zq0, pair, sq0)
     b_q0.start()
-    b_kv.forward()
     a_q1.finish_in()
     a_d.start()
     for pair in range(4):
         pack_pair(hots, zq1, pair, sq1)
     b_q1.start()
-    b_q0.forward()
 
     b_kv.finish_in()
     total = jnp.zeros((8, 768), F32)
@@ -261,7 +248,6 @@
         device_id=(here.dp, here.partner()), device_id_type=MESH,
     )
     swap.start()
-    b_q1.forward()
     swapped = kv_ref.at[1 - parity]
     pltpu.make_async_remote_copy(
         src_ref=swapped, dst_ref=swapped, send_sem=swap_s, recv_sem=swap_r,
@@ -292,9 +278,10 @@
             jax.ShapeDtypeStruct((16, TOK, 256), BF16),
             jax.ShapeDtypeStruct((16, TOK, 512), BF16),
         ),
-        in_specs=[VMEM] * 4 + [ANY] * 2,
+        in_specs=[VMEM] + [HBM] * 4,
         out_specs=(VMEM,) * 5 + (ANY, ANY, VMEM),
         scratch_shapes=[
+            DMA((8,)),
             pltpu.VMEM((8, TOK), jnp.int32),
             pltpu.VMEM((8, 8, TOK), jnp.int32),
             pltpu.VMEM((TOK, 1024), BF16),
@@ -311,10 +298,10 @@
             DMA,
         ]
         + Column.scratch() * 5
-        + Plane.scratch(TOK + 32, D) + Plane.scratch(TOK, 256) + Plane.scratch(TOK, 256),
+        + Plane.scratch() * 3,
         compiler_params=pltpu.CompilerParams(collective_id=0, has_side_effects=True, vmem_limit_bytes=44 << 20),
         name="bring_in",
-    )(destination.reshape(1, TOK), destination.reshape(TOK, 1), keys, values, queries, grad_out)
+    )(destination.reshape(1, TOK), keys, values, queries, grad_out)
 
 
 def tiles():
@@ -364,7 +351,7 @@
     b_d = Plane(here, pd_ref, gd_ref, sems)
     greet(here, plane=True)
     b_d.start()
-    end = end_ref[0]
+    end = end_ref[here.dp, 0]
     for pair in range(4):
         hot = hot_of(place_ref, pair)
         for n, got in enumerate((gq0_ref, gq1_ref)):
@@ -376,7 +363,6 @@
     def _(h):
         forward_head(h, end, q_ref, kv_ref, vt_ref, o_ref, lse_ref)
 
-    b_d.forward()
 
     @pl.loop(2, 4)
     def _(h):
@@ -389,7 +375,7 @@
     b_d.finish_out()
 
 
-def forward(end, place, kv, vt, gq0, gq1, pd):
+def forward(lengths, place, kv, vt, gq0, gq1, pd):
     return pl.pallas_call(
         forward_kernel,
         out_shape=(
@@ -401,10 +387,10 @@
         ),
         in_specs=[SMEM] + [VMEM] * 5 + [ANY],
         out_specs=(VMEM,) * 4 + (ANY,),
-        scratch_shapes=Plane.scratch(TOK, 512),
+        scratch_shapes=Plane.scratch(),
         compiler_params=pltpu.CompilerParams(collective_id=1, has_side_effects=True, vmem_limit_bytes=44 << 20),
         name="forward",
-    )(end, place, kv, vt, gq0, gq1, pd)
+    )(lengths, place, kv, vt, gq0, gq1, pd)
 
 
 def backward_head(h, end, q_ref, d_ref, o_ref, lse_ref, kv_ref, kt_ref, g_ref, gq_ref):
@@ -430,27 +416,21 @@
 
 
 def backward_kernel(end_ref, place_ref, kv_ref, kt_ref, gd_ref, q_ref, o_ref, lse_ref, po_ref,
-                    pq_ref, pkv_ref, go_ref,
+                    pq0_ref, pq1_ref, pkv_ref, go_ref,
                     d_ref, gq_ref, g_ref, landed, swap_s, swap_r, *sems):
     here = Here()
     parity = here.ctx % 2
-    b_o = Plane(here, po_ref, go_ref, sems)
+    b_o = Plane(here, po_ref, go_ref, sems, order=(11, 12, 13, 14, 9, 10, 5, 6, 7, 8, 1, 2, 3, 4, 0))
     greet(here, plane=True, partner=True)
     b_o.start()
-    end = end_ref[0]
+    end = end_ref[here.dp, 0]
     g_ref[...] = jnp.zeros_like(g_ref)
     for pair in range(4):
         x = dot(hot_of(place_ref, pair), gd_ref[:, 48 * pair : 48 * pair + 48].reshape(768, 512)).astype(BF16)
         for h in range(4):
             d_ref[h, 384 * pair : 384 * pair + 384] = x[:, h * D : h * D + D]
 
-    @pl.loop(0, 2)
-    def _(h):
-        backward_head(h, end, q_ref, d_ref, o_ref, lse_ref, kv_ref, kt_ref, g_ref, gq_ref)
-
-    b_o.forward()
-
-    @pl.loop(2, 4)
+    @pl.loop(0, 4)
     def _(h):
         backward_head(h, end, q_ref, d_ref, o_ref, lse_ref, kv_ref, kt_ref, g_ref, gq_ref)
 
@@ -461,7 +441,9 @@
     swap.start()
     for pair in range(4):
         x = jnp.concatenate([gq_ref[h, 384 * pair : 384 * pair + 384] for h in range(4)], axis=1)
-        pq_ref[:, 48 * pair : 48 * pair + 48] = dot(hot_of(place_ref, pair), x, TN).astype(BF16).reshape(16, 48, 512)
+        packed = dot(hot_of(place_ref, pair), x, TN).astype(BF16).reshape(16, 48, 512)
+        pq0_ref[:, 48 * pair : 48 * pair + 48] = packed[:, :, :256]
+        pq1_ref[:, 48 * pair : 48 * pair + 48] = packed[:, :, 256:]
     swap.wait_recv()
     factor = jnp.where(parity == 0, SCALE, 1.0).astype(F32)
     for pair in range(4):
@@ -473,16 +455,17 @@
     b_o.finish_out()
 
 
-def backward(end, place, kv, kt, gd, q, o, lse, po):
+def backward(lengths, place, kv, kt, gd, q, o, lse, po):
     return pl.pallas_call(
         backward_kernel,
         out_shape=(
-            jax.ShapeDtypeStruct((16, TOK, 512), BF16),
+            jax.ShapeDtypeStruct((16, TOK, 256), BF16),
+            jax.ShapeDtypeStruct((16, TOK, 256), BF16),
             jax.ShapeDtypeStruct((16, TOK, D), BF16),
             jax.ShapeDtypeStruct((16, TOK, 512), BF16),
         ),
         in_specs=[SMEM] + [VMEM] * 7 + [ANY],
-        out_specs=(VMEM, VMEM, ANY),
+        out_specs=(VMEM, VMEM, VMEM, ANY),
         scratch_shapes=[
             pltpu.VMEM((4, 1536, D), BF16),
             pltpu.VMEM((4, 1536, D), BF16),
@@ -491,24 +474,27 @@
             DMA,
             DMA,
         ]
-        + Plane.scratch(TOK, 512),
+        + Plane.scratch(),
         compiler_params=pltpu.CompilerParams(collective_id=2, has_side_effects=True, vmem_limit_bytes=44 << 20),
         name="backward",
-    )(end, place, kv, kt, gd, q, o, lse, po)
-
-
-def out_kernel(slots_ref, go_ref, pq_ref, pkv_ref, oo_ref, oq_ref, ok_ref, ov_ref,
-               gq, gkv, zo, zq, zkv, okv, hots, *sems):
+    )(lengths, place, kv, kt, gd, q, o, lse, po)
+
+
+def out_kernel(slots_ref, go_ref, pq0_ref, pq1_ref, pkv_ref, oo_ref, oq_ref, ok_ref, ov_ref,
+               gq0, gq1, gkv, zo, zq0, zq1, zkv, okv, hots, *sems):
     here = Here()
-    cs = [sems[3 * i : 3 * i + 3] for i in range(3)]
-    ps = [sems[9 + 8 * i : 17 + 8 * i] for i in range(2)]
-    b_q = Plane(here, pq_ref, gq, ps[0])
-    b_kv = Plane(here, pkv_ref, gkv, ps[1])
+    cs = [sems[3 * i : 3 * i + 3] for i in range(4)]
+    ps = [sems[12 + 3 * i : 15 + 3 * i] for i in range(3)]
+    b_q0 = Plane(here, pq0_ref, gq0, ps[0])
+    b_q1 = Plane(here, pq1_ref, gq1, ps[1])
+    b_kv = Plane(here, pkv_ref, gkv, ps[2])
     a_o = Column(here, lambda p: zo.at[p], lambda p: oo_ref.at[:, cols(p * 512, 512)], cs[0])
-    a_q = Column(here, lambda p: zq.at[p], lambda p: oq_ref.at[:, cols(p * 512, 512)], cs[1])
-    a_kv = Column(here, lambda p: zkv.at[p], lambda p: okv.at[:, cols(p * D, D)], cs[2])
+    a_q0 = Column(here, lambda p: zq0.at[p], lambda p: oq_ref.at[:, cols(p * 512, 256)], cs[1])
+    a_q1 = Column(here, lambda p: zq1.at[p], lambda p: oq_ref.at[:, cols(p * 512 + 256, 256)], cs[2])
+    a_kv = Column(here, lambda p: zkv.at[p], lambda p: okv.at[:, cols(p * D, D)], cs[3])
     greet(here, plane=True, column=True)
-    b_q.start()
+    b_q0.start()
+    b_q1.start()
     b_kv.start()
     slot_c = jnp.transpose(slots_ref[...])
 
@@ -522,25 +508,27 @@
         hots[c] = jnp.where(iota((TOK, 768), 1).astype(F32) == slot_c[:, c : c + 1], 1.0, 0.0).astype(BF16)
     unpack(go_ref, zo)
     a_o.start()
-    b_q.forward()
-    b_kv.forward()
-    b_q.finish_in()
-    unpack(gq, zq)
-    a_q.start()
+    b_q0.finish_in()
+    unpack(gq0, zq0)
+    a_q0.start()
+    b_q1.finish_in()
+    unpack(gq1, zq1)
+    a_q1.start()
     b_kv.finish_in()
     unpack(gkv, zkv)
     a_kv.start()
+    a_o.finish_in()
+    a_q0.finish_in()
+    a_q1.finish_in()
     a_kv.finish_in()
     for z in range(4):
         ok_ref[:, z * D : z * D + D] = okv[:, 2 * z * D : 2 * z * D + D]
         ov_ref[:, z * D : z * D + D] = okv[:, 2 * z * D + D : 2 * z * D + 2 * D]
-    a_o.finish_in()
-    a_q.finish_in()
-    for c in (b_q, b_kv, a_o, a_q, a_kv):
+    for c in (b_q0, b_q1, b_kv, a_o, a_q0, a_q1, a_kv):
         c.finish_out()
 
 
-def take_back(slots, go, pq, pkv):
+def take_back(slots, go, pq0, pq1, pkv):
     return pl.pallas_call(
         out_kernel,
         out_shape=(
@@ -549,30 +537,31 @@
             jax.ShapeDtypeStruct((TOK, 512), BF16),
             jax.ShapeDtypeStruct((TOK, 512), BF16),
         ),
-        in_specs=[VMEM, VMEM, ANY, ANY],
+        in_specs=[VMEM, VMEM, ANY, ANY, ANY],
         out_specs=(ANY, ANY, VMEM, VMEM),
         scratch_shapes=[
-            pltpu.VMEM((16, TOK, 512), BF16),
+            pltpu.VMEM((16, TOK, 256), BF16),
+            pltpu.VMEM((16, TOK, 256), BF16),
             pltpu.VMEM((16, TOK, D), BF16),
             pltpu.VMEM((8, TOK, 512), BF16),
-            pltpu.VMEM((8, TOK, 512), BF16),
+            pltpu.VMEM((8, TOK, 256), BF16),
+            pltpu.VMEM((8, TOK, 256), BF16),
             pltpu.VMEM((8, TOK, D), BF16),
             pltpu.VMEM((TOK, 1024), BF16),
             pltpu.VMEM((8, TOK, 768), BF16),
         ]
-        + Column.scratch() * 3
-        + Plane.scratch(TOK, 512) + Plane.scratch(TOK, D),
+        + Column.scratch() * 4
+        + Plane.scratch() * 3,
         compiler_params=pltpu.CompilerParams(collective_id=3, has_side_effects=True, vmem_limit_bytes=44 << 20),
         name="take_back",
-    )(slots, go, pq, pkv)
+    )(slots, go, pq0, pq1, pkv)
 
 
 def local(queries, keys, values, grad_out, destination, lengths):
-    end = lax.dynamic_slice(lengths, (lax.axis_index("dp"), 0), (1, 1)).reshape(1)
     slots, place, kv, kt, vt, gq0, gq1, pd = bring_in(destination, keys, values, queries, grad_out)
-    q, o, lse, po, gd = forward(end, place, kv, vt, gq0, gq1, pd)
-    pq, pkv, go = backward(end, place, kv, kt, gd, q, o, lse, po)
-    return take_back(slots, go, pq, pkv)
+    q, o, lse, po, gd = forward(lengths, place, kv, vt, gq0, gq1, pd)
+    pq0, pq1, pkv, go = backward(lengths, place, kv, kt, gd, q, o, lse, po)
+    return take_back(slots, go, pq0, pq1, pkv)
 
 
 def solution(mesh):

time: 267 us -> 245 us (0.918)
  Pallas kernels: 249 us -> 230 us
  local copies, waits for them, and re-layouts: 14.5 us -> 9.74 us
    pallas_call x1, Pallas kernels: 80.3 us -> 64.3 us  [take_back(): pl.pallas_call(out_kernel, out_shape=(jax.ShapeDtypeStruct((TOK, 4096), B...]
    pallas_call x1, Pallas kernels: 52.1 us -> 44.7 us  [backward(): pl.pallas_call(backward_kernel, out_shape=(jax.ShapeDtypeStruct((16, TOK,...]
    unnamed x20 -> x15, local copies, waits for them, and re-layouts: 13.2 us -> 9.74 us
    pallas_call x1, Pallas kernels: 67.5 us -> 70.2 us  [bring_in(): pl.pallas_call(in_kernel, out_shape=(jax.ShapeDtypeStruct((8, TOK), F32),...]
where the time goes in v2:
time: 245 us; the launch traced here: 241 us
  Pallas kernels  230 us (94%)
  local copies, waits for them, and re-layouts  9.74 us (4%)
    pallas_call x1, Pallas kernels, bring_in(): pl.pallas_call(in_kernel, out_shape=(jax.ShapeDtypeStruct((8, TOK), F32),...  70.2 us
    pallas_call x1, Pallas kernels, take_back(): pl.pallas_call(out_kernel, out_shape=(jax.ShapeDtypeStruct((TOK, 4096), B...  64.3 us
    pallas_call x1, Pallas kernels, forward(): pl.pallas_call(forward_kernel, out_shape=(jax.ShapeDtypeStruct((4, 1536,...  51 us
    pallas_call x1, Pallas kernels, backward(): pl.pallas_call(backward_kernel, out_shape=(jax.ShapeDtypeStruct((16, TOK,...  44.7 us
    unnamed x15, local copies, waits for them, and re-layouts  9.74 us

profile of v2, /device:TPU:16, one launch (start us, length us, event | category | flops | bytes accessed | tf_op | source)
XLA Modules:
  0.0 240.7 jit_solution(7056053062176378885)
XLA Ops:
  0.6 0.8 copy.11.end_ref
  1.4 0.0 copy-start
  1.4 1.4 copy-done
  2.8 0.0 copy-start.1
  2.8 1.4 copy-done.1
  4.2 0.0 copy-start.2
  4.2 0.9 copy-done.2
  5.1 0.0 copy-start.3
  5.1 0.9 copy-done.3
  6.1 0.0 copy-start.4
  6.1 0.7 copy-done.4
  6.7 70.2 %bring_in.1 = (f32[8,192]{1,0:T(8,128)S(1)}, f32[8,768]{1,0:T(8,128)S(1)}, bf16[2,1536,128]{2,1,0:T(8,128)(2,1)S(1)}, bf16[128,1536]{1,0:T(8,128)(2,1)S(1)}, bf1...) custom-call(s32[1,192]{1,0:T(1,128)S(1)} %bitcast.1, ...), custom_call_target="tpu_custom_call" | custom-call | tf_op jit(solution)/shard_map/bring_in/pallas_call | solution.py:269
  77.0 51.0 %forward.1 = (bf16[4,1536,128]{2,1,0:T(8,128)(2,1)S(1)}, bf16[4,1536,128]{2,1,0:T(8,128)(2,1)S(1)}, f32[4,1,1536]{2,1,0:T(1,128)S(1)}, bf16[16,192,512]{2,1,0:T(8,128)(2,1)}, bf16[16,192,512]{2,1,0:T(8,128)(2,1)}) custom-call(s32[16,2]{1,0:T(8,128)S(1)} %copy.11.end_ref, f32[8,768]{1,0:T(8,128)S(1)} %get-tuple-element.22.place_ref, ...), custom_call_target="tpu_custom_call" | custom-call | tf_op jit(solution)/shard_map/forward/pallas_call | solution.py:379
  128.0 44.7 %backward.1 = (bf16[16,192,256]{2,1,0:T(8,128)(2,1)S(1)}, bf16[16,192,256]{2,1,0:T(8,128)(2,1)S(1)}, bf16[16,192,128]{2,1,0:T(8,128)(2,1)S(1)}, bf16[16,192,512]{2,1,0:T(8,128)(2,1)}) custom-call(s32[16,2]{1,0:T(8,128)S(1)} %copy.11.end_ref, f32[8,768]{1,0:T(8,128)S(1)} %get-tuple-element.22.place_ref, bf16[2,1536,128]{2,1,0:T(8,128)(2,1)S(1)} %get-tuple-element.23.kv_ref, ...), custom_call_target="tpu_custom_call" | custom-call | tf_op jit(solution)/shard_map/backward/pallas_call | solution.py:459
  172.7 64.3 %take_back.1 = (bf16[192,4096]{1,0:T(8,128)(2,1)S(1)}, bf16[192,4096]{1,0:T(8,128)(2,1)S(1)}, bf16[192,512]{1,0:T(8,128)(2,1)S(1)}, bf16[192,512]{1,0:T(8,128)(2,1)S(1)}) custom-call(f32[8,192]{1,0:T(8,128)S(1)} %get-tuple-element.21.slots_ref, bf16[16,192,512]{2,1,0:T(8,128)(2,1)} %get-tuple-element.34.go_ref, ...), custom_call_target="tpu_custom_call" | custom-call | tf_op jit(solution)/shard_map/take_back/pallas_call | solution.py:532
  237.0 1.1 copy.16
  238.2 1.1 copy.17
  239.3 0.7 copy.18
  240.0 0.7 copy.19
Async XLA Ops:
  1.4 1.4 copy-start
  2.8 1.4 copy-start.1
  4.2 0.9 copy-start.2
  5.1 0.9 copy-start.3
  6.1 0.7 copy-start.4

commit v3 on v0

v3 whole, which is shorter than its diff:
```python
import functools
import math

import jax
import jax.numpy as jnp
from jax import lax
from jax.experimental import pallas as pl
from jax.experimental.pallas import tpu as pltpu
from jax.sharding import PartitionSpec as P

D = 128
TOK = 192
CAP = 24
F32 = jnp.float32
BF16 = jnp.bfloat16
MESH = pl.DeviceIdType.MESH
VMEM = pl.BlockSpec(memory_space=pltpu.VMEM)
SMEM = pl.BlockSpec(memory_space=pltpu.SMEM)
HBM = pl.BlockSpec(memory_space=pltpu.HBM)
DMA = pltpu.SemaphoreType.DMA
NN = (((1,), (0,)), ((), ()))
NT = (((1,), (1,)), ((), ()))
TN = (((0,), (0,)), ((), ()))
TILE = 256
SCALE = 1.0 / math.sqrt(D)
EXP2 = SCALE * math.log2(math.e)


def dot(a, b, dims=NN):
    return lax.dot_general(a, b, dims, preferred_element_type=F32)


def iota(shape, axis):
    return lax.broadcasted_iota(jnp.int32, shape, axis)


def group_of(dest):
    return ((dest >> 9) * 43) >> 7


def place_of(dest):
    return dest - 192 * (((dest >> 6) * 171) >> 9)


STEPS = [(1, 0), (-1, 0), (0, 1), (0, -1), (2, 0), (0, 2), (1, 1), (-1, -1), (1, -1), (-1, 1),
         (2, 1), (1, 2), (2, -1), (-1, 2), (2, 2)]
INWARD = (0, 3, 1, 2)
OUTWARD = (2, 1, 3, 0)


class Here:
    def __init__(self):
        self.dp = lax.axis_index("dp")
        self.ctx = lax.axis_index("ctx")
        self.x, self.y = self.dp // 4, self.dp % 4
        self.z, self.core = self.ctx // 2, self.ctx % 2

    def at(self, dx, dy):
        return ((self.x + (dx + 4)) % 4) * 4 + (self.y + (dy + 4)) % 4

    def chip(self, dz):
        return (self.z + (dz + 4)) % 4

    def peer(self, dz, other):
        return self.chip(dz) * 2 + (self.core + other) % 2


def greet(here):
    barrier = pltpu.get_barrier_semaphore()
    who = [(here.at(*step), here.ctx) for step in STEPS] + [(here.dp, here.peer(*step)) for step in COLUMN[1:]]
    for device in who:
        pl.semaphore_signal(barrier, inc=1, device_id=device, device_id_type=MESH)
    pl.semaphore_wait(barrier, len(who))


def remote(src, dst, send_sem, recv_sem, device):
    return pltpu.make_async_remote_copy(
        src_ref=src, dst_ref=dst, send_sem=send_sem, recv_sem=recv_sem, device_id=device, device_id_type=MESH
    )


class Plane:
    @staticmethod
    def scratch(parts):
        return [DMA((parts, 15)), DMA((parts, 15)), DMA((parts,))]

    def __init__(self, here, send, recv, scratch, rows):
        self.here, self.send, self.recv, self.rows = here, send, recv, rows
        self.send_s, self.recv_s, self.own_s = scratch
        self.begun = []

    def own(self, part):
        me, rows = self.here.dp, self.rows(part)
        return pltpu.make_async_copy(self.send.at[me, rows], self.recv.at[me, rows], self.own_s.at[part])

    def start(self, part=0):
        rows = self.rows(part)
        for i, (dx, dy) in enumerate(STEPS):
            to = self.here.at(dx, dy)
            c = remote(self.send.at[to, rows], self.recv.at[self.here.dp, rows],
                       self.send_s.at[part, i], self.recv_s.at[part, i], (to, self.here.ctx))
            c.start()
            self.begun.append(c)
        self.own(part).start()

    def finish_in(self, part=0):
        rows = self.rows(part)
        for i, (dx, dy) in enumerate(STEPS):
            source = self.here.at(-dx, -dy)
            landing = self.recv.at[source, rows]
            remote(landing, landing, self.send_s.at[part, i], self.recv_s.at[part, i], (source, self.here.ctx)).wait_recv()
        self.own(part).wait()

    def finish_out(self):
        for c in self.begun:
            c.wait_send()


COLUMN = [(0, 0), (0, 1), (1, 0), (1, 1), (3, 0), (3, 1), (2, 0), (2, 1)]


class Column:
    @staticmethod
    def scratch():
        return [DMA((8,)), DMA((8,)), DMA]

    def __init__(self, here, source, target, scratch):
        self.here, self.source, self.target = here, source, target
        self.send_s, self.recv_s, self.own_s = scratch
        self.own = pltpu.make_async_copy(source(here.ctx), target(here.ctx), self.own_s)
        self.begun = []

    def start_chip(self, dz):
        for other in range(2):
            if (dz, other) == (0, 0):
                self.own.start()
                continue
            to, n = self.here.peer(dz, other), 2 * dz + other
            c = remote(self.source(to), self.target(self.here.ctx), self.send_s.at[n], self.recv_s.at[n], (self.here.dp, to))
            c.start()
            self.begun.append(c)

    def start(self):
        for dz in (0, 1, 3, 2):
            self.start_chip(dz)

    def finish_chip(self, dz):
        for other in range(2):
            n = 2 * ((4 - dz) % 4) + other
            if n == 0:
                self.own.wait()
                continue
            origin = self.here.peer(dz, other)
            landing = self.target(origin)
            remote(landing, landing, self.send_s.at[n], self.recv_s.at[n], (self.here.dp, origin)).wait_recv()

    def finish_in(self):
        for dz in range(4):
            self.finish_chip(dz)

    def finish_out(self):
        for c in self.begun:
            c.wait_send()


def cols(start, width):
    return pl.ds(pl.multiple_of(start, 128), width)


def hot_of(place_ref, pair):
    return jnp.where(place_ref[pl.ds(pair, 1)] == (iota((384, 768), 0) + 1).astype(F32), 1.0, 0.0).astype(BF16)


def rows48(pair):
    return pl.ds(pl.multiple_of(48 * pair, 16), 48)


def rows384(pair):
    return pl.ds(pl.multiple_of(384 * pair, 128), 384)


def pack_pair(hots, z_ref, pair, out_ref):
    x = dot(hots[2 * pair], z_ref[2 * pair]) + dot(hots[2 * pair + 1], z_ref[2 * pair + 1])
    out_ref[:, rows48(pair)] = x.astype(BF16).reshape(16, 48, z_ref.shape[2])


def unpack_pair(backs, got, pair, z_ref):
    x = got[:, rows48(pair)].reshape(768, got.shape[2])
    for c in range(2):
        z_ref[2 * pair + c] = dot(backs[2 * pair + c], x).astype(BF16)


def regroup(place_ref, got, pair):
    return dot(hot_of(place_ref, pair), got[:, rows48(pair)].reshape(768, got.shape[2]))


def return_pair(place_ref, x, pair, out_ref):
    packed = dot(hot_of(place_ref, pair), x, TN).astype(BF16)
    out_ref[:, rows48(pair)] = packed.reshape(16, 48, x.shape[1])


def tiles():
    for j in range(6):
        low = 0 if j < 4 else 512
        yield j, list(range(low, (j + 1) * TILE, TILE))


def allowed(j, k, end):
    diagonal, mixed = k == j * TILE, j >= 2
    if not diagonal and not mixed:
        return None
    kp = k + iota((TILE, TILE), 0)
    qp = j * TILE + iota((1, TILE), 1)
    mask = None
    if mixed:
        mask = kp >= jnp.where(qp >= end, end, 0)
    if diagonal:
        causal = kp <= qp
        mask = causal if mask is None else mask & causal
    return mask


def forward_head(h, end, q_ref, kv_ref, vt_ref, o_ref, lse_ref):
    for j, ks in tiles():
        rows = slice(j * TILE, j * TILE + TILE)
        q = q_ref[h, rows]
        scores = []
        for k in ks:
            s = dot(kv_ref[0, k : k + TILE], q, NT)
            mask = allowed(j, k, end)
            scores.append(s if mask is None else jnp.where(mask, s, -jnp.inf))
        top = jnp.max(functools.reduce(jnp.maximum, scores), axis=0, keepdims=True)
        expo = [jnp.exp2((s - top) * EXP2) for s in scores]
        total = jnp.sum(functools.reduce(jnp.add, expo), axis=0, keepdims=True)
        inverse = 1.0 / total
        att = jnp.zeros((D, TILE), F32)
        for k, e in zip(ks, expo):
            att += dot(vt_ref[:, k : k + TILE], (e * inverse).astype(BF16))
        o_ref[h, rows] = jnp.transpose(att).astype(BF16)
        lse_ref[h, :, rows] = top * EXP2 + jnp.log2(total)


def backward_head(h, end, q_ref, d_ref, o_ref, lse_ref, kv_ref, kt_ref, g_ref, gq_ref):
    for j, ks in tiles():
        rows = slice(j * TILE, j * TILE + TILE)
        q, d = q_ref[h, rows], d_ref[h, rows]
        product = d.astype(F32) * o_ref[h, rows].astype(F32)
        delta = jnp.sum(jnp.transpose(product), axis=0, keepdims=True)
        lse = lse_ref[h, :, rows]
        gq = jnp.zeros((D, TILE), F32)
        for k in ks:
            keys = slice(k, k + TILE)
            p = jnp.exp2(dot(kv_ref[0, keys], q, NT) * EXP2 - lse)
            mask = allowed(j, k, end)
            if mask is not None:
                p = jnp.where(mask, p, 0.0)
            dp = dot(kv_ref[1, keys], d, NT)
            ds = (p * (dp - delta)).astype(BF16)
            g_ref[1, keys] += dot(p.astype(BF16), d)
            g_ref[0, keys] += dot(ds, q)
            gq += dot(kt_ref[:, keys], ds)
        gq_ref[h, rows] = jnp.transpose(gq * SCALE).astype(BF16)


def whole_kernel(lengths_ref, row_ref, k_ref, v_ref, qin_ref, din_ref, oo_ref, oq_ref, ok_ref, ov_ref,
                 load, info, infos, kvs, zkv, zq, zd, hots, backs, place,
                 skv, rkv, sq, rq, sd, rd, kv, kt, vt, q, o, d, gq, lse, g, landed,
                 so, ro, sg, rg, skg, rkg, zo, zg, zkg, okv, swap_s, swap_r, *sems):
    here = Here()
    core = here.core
    every = lambda part: pl.ds(0, TOK + 32)
    plain = lambda part: pl.ds(0, TOK)
    chunk = lambda part: rows48(here.chip(part))
    cs = [sems[3 * i : 3 * i + 3] for i in range(7)]
    ps = [sems[21 + 3 * i : 24 + 3 * i] for i in range(6)]
    a_info = Column(here, lambda p: info, lambda p: infos.at[p], cs[0])
    a_kv = Column(here, lambda p: kvs.at[:, cols(p * D, D)], lambda p: zkv.at[p], cs[1])
    a_q = Column(here, lambda p: qin_ref.at[:, cols(p * 512, 512)], lambda p: zq.at[p], cs[2])
    a_d = Column(here, lambda p: din_ref.at[:, cols(p * 512, 512)], lambda p: zd.at[p], cs[3])
    a_o = Column(here, lambda p: zo.at[p], lambda p: oo_ref.at[:, cols(p * 512, 512)], cs[4])
    a_g = Column(here, lambda p: zg.at[p], lambda p: oq_ref.at[:, cols(p * 512, 512)], cs[5])
    a_kg = Column(here, lambda p: zkg.at[p], lambda p: okv.at[:, cols(p * D, D)], cs[6])
    b_kv = Plane(here, skv, rkv, ps[0], every)
    b_kg = Plane(here, skg, rkg, ps[1], plain)
    b_q = Plane(here, sq, rq, ps[2], chunk)
    b_d = Plane(here, sd, rd, ps[3], chunk)
    b_o = Plane(here, so, ro, ps[4], chunk)
    b_g = Plane(here, sg, rg, ps[5], chunk)

    loads = []
    for z in range(4):
        for e, ref in enumerate((k_ref, v_ref)):
            to = kvs.at[:, pl.ds((2 * z + e) * D, D)]
            loads.append(pltpu.make_async_copy(ref.at[:, pl.ds(z * D, D)], to, load.at[2 * z + e]))
    for c in loads:
        c.start()
    dest_r = row_ref[...]
    g_r = group_of(dest_r)
    g_c = jnp.transpose(jnp.broadcast_to(g_r.astype(F32), (8, TOK)))[:, 0:1]
    same = (g_r.astype(F32) == g_c) & (iota((TOK, TOK), 0) < iota((TOK, TOK), 1))
    rank = jnp.sum(jnp.where(same, 1.0, 0.0), axis=0, keepdims=True).astype(jnp.int32) + CAP * core
    which = iota((8, TOK), 0)
    info[...] = jnp.where(
        which == 0, g_r * 48 + rank, jnp.where(which == 1, place_of(dest_r) + 1, jnp.where(which == 2, g_r, rank))
    )
    for c in loads:
        c.wait()

    greet(here)
    a_info.start()
    a_kv.start()
    a_q.start()
    a_info.finish_in()
    which = iota((16, 32, D), 1)
    tail = jnp.zeros((16, 32, D), F32)
    for pair in range(4):
        laid = jnp.zeros((16, D), F32)
        for c in (2 * pair, 2 * pair + 1):
            hots[c] = jnp.where(iota((768, TOK), 0) == infos[c, 0:1], 1.0, 0.0).astype(BF16)
            named = jnp.where(iota((16, TOK), 0) == infos[c, 2:3], infos[c, 1:2].astype(F32), 0.0).astype(BF16)
            laned = jnp.where(iota((D, TOK), 0) == infos[c, 3:4], 1.0, 0.0).astype(BF16)
            laid += dot(named, laned, NT)
        tail = jnp.where(which == pair, laid.reshape(16, 1, D), tail)
    a_kv.finish_in()
    for pair in range(4):
        pack_pair(hots, zkv, pair, skv)
    skv[:, TOK:] = tail.astype(BF16)
    b_kv.start()
    for part in INWARD:
        a_q.finish_chip(part)
        pack_pair(hots, zq, here.chip(part), sq)
        b_q.start(part)
    a_d.start()
    slot_c = jnp.transpose(jnp.concatenate([infos[c, 0:1].astype(F32) for c in range(8)], axis=0))
    for c in range(8):
        backs[c] = jnp.where(iota((TOK, 768), 1).astype(F32) == slot_c[:, c : c + 1], 1.0, 0.0).astype(BF16)

    b_kv.finish_in()
    total = jnp.zeros((8, 768), F32)
    for s in range(16):
        mine = jnp.concatenate([rkv[s, TOK : TOK + 16].astype(F32)[:8], jnp.zeros((8, 640), F32)], axis=1)
        total += mine if s == 0 else pltpu.roll(mine, 48 * s, 1)
    odd = (iota((8, 768), 1) % 48) >= CAP
    place[...] = jnp.where(odd & (total > 0.0), total + 192.0, total)
    for pair in range(4):
        kv[core, rows384(pair)] = regroup(place, rkv, pair).astype(BF16)
    partner = (here.dp, here.peer(0, 1))
    swap = remote(kv.at[core], kv.at[core], swap_s.at[0], swap_r.at[0], partner)
    swap.start()
    for part in INWARD:
        a_d.finish_chip(part)
        pack_pair(hots, zd, here.chip(part), sd)
        b_d.start(part)
    swapped = kv.at[1 - core]
    remote(swapped, swapped, swap_s.at[0], swap_r.at[0], partner).wait_recv()
    kt[...] = jnp.transpose(kv[0].astype(F32)).astype(BF16)
    vt[...] = jnp.transpose(kv[1].astype(F32)).astype(BF16)

    end = lengths_ref[0, here.dp]
    for part in INWARD:
        b_q.finish_in(part)
        pair = here.chip(part)
        x = regroup(place, rq, pair).astype(BF16)
        for h in range(4):
            q[h, rows384(pair)] = x[:, h * D : h * D + D]

    @pl.loop(0, 4)
    def _(h):
        forward_head(h, end, q, kv, vt, o, lse)

    for part in OUTWARD:
        pair = here.chip(part)
        return_pair(place, jnp.concatenate([o[h, rows384(pair)] for h in range(4)], axis=1), pair, so)
        b_o.start(part)

    swap.wait_send()
    g[...] = jnp.zeros_like(g)
    for part in INWARD:
        b_d.finish_in(part)
        pair = here.chip(part)
        x = regroup(place, rd, pair).astype(BF16)
        for h in range(4):
            d[h, rows384(pair)] = x[:, h * D : h * D + D]

    @pl.loop(0, 4)
    def _(h):
        backward_head(h, end, q, d, o, lse, kv, kt, g, gq)

    swap = remote(g.at[1 - core], landed, swap_s.at[1], swap_r.at[1], partner)
    swap.start()

    def give(part):
        pair = here.chip(part)
        return_pair(place, jnp.concatenate([gq[h, rows384(pair)] for h in range(4)], axis=1), pair, sg)
        b_g.start(part)

    give(OUTWARD[0])
    give(OUTWARD[1])
    swap.wait_recv()
    factor = jnp.where(core == 0, SCALE, 1.0).astype(F32)
    for pair in range(4):
        rows = rows384(pair)
        return_pair(place, ((g[core, rows] + landed[rows]) * factor).astype(BF16), pair, skg)
    b_kg.start()
    for part in OUTWARD:
        b_o.finish_in(part)
        unpack_pair(backs, ro, here.chip(part), zo)
        a_o.start_chip(part)
    give(OUTWARD[2])
    give(OUTWARD[3])
    for part in OUTWARD[:2]:
        b_g.finish_in(part)
        unpack_pair(backs, rg, here.chip(part), zg)
        a_g.start_chip(part)
    b_kg.finish_in()
    for pair in range(4):
        unpack_pair(backs, rkg, pair, zkg)
    a_kg.start()
    for part in OUTWARD[2:]:
        b_g.finish_in(part)
        unpack_pair(backs, rg, here.chip(part), zg)
        a_g.start_chip(part)
    a_kg.finish_in()
    for z in range(4):
        ok_ref[:, z * D : z * D + D] = okv[:, 2 * z * D : 2 * z * D + D]
        ov_ref[:, z * D : z * D + D] = okv[:, 2 * z * D + D : 2 * z * D + 2 * D]
    a_o.finish_in()
    a_g.finish_in()
    swap.wait_send()
    for c in (a_info, a_kv, a_q, a_d, a_o, a_g, a_kg, b_kv, b_kg, b_q, b_d, b_o, b_g):
        c.finish_out()


def local(queries, keys, values, grad_out, destination, lengths):
    slots, wide = (16, TOK, 512), (8, TOK, 512)
    scratch = [
        ((8, TOK), jnp.int32), ((8, 8, TOK), jnp.int32), ((TOK, 1024), BF16), ((8, TOK, D), BF16), (wide, BF16), (wide, BF16),
        ((8, 768, TOK), BF16), ((8, TOK, 768), BF16), ((8, 768), F32),
        ((16, TOK + 32, D), BF16), ((16, TOK + 32, D), BF16), (slots, BF16), (slots, BF16), (slots, BF16), (slots, BF16),
        ((2, 1536, D), BF16), ((D, 1536), BF16), ((D, 1536), BF16),
        ((4, 1536, D), BF16), ((4, 1536, D), BF16), ((4, 1536, D), BF16), ((4, 1536, D), BF16), ((4, 1, 1536), F32),
        ((2, 1536, D), F32), ((1536, D), F32),
        (slots, BF16), (slots, BF16), (slots, BF16), (slots, BF16), ((16, TOK, D), BF16), ((16, TOK, D), BF16),
        (wide, BF16), (wide, BF16), ((8, TOK, D), BF16), ((TOK, 1024), BF16),
    ]
    return pl.pallas_call(
        whole_kernel,
        out_shape=(
            jax.ShapeDtypeStruct((TOK, 4096), BF16),
            jax.ShapeDtypeStruct((TOK, 4096), BF16),
            jax.ShapeDtypeStruct((TOK, 512), BF16),
            jax.ShapeDtypeStruct((TOK, 512), BF16),
        ),
        in_specs=[SMEM, VMEM] + [HBM] * 4,
        out_specs=(HBM, HBM, VMEM, VMEM),
        scratch_shapes=[DMA((8,))]
        + [pltpu.VMEM(shape, dtype) for shape, dtype in scratch]
        + [DMA((2,)), DMA((2,))]
        + Column.scratch() * 7
        + Plane.scratch(1) * 2 + Plane.scratch(4) * 4,
        compiler_params=pltpu.CompilerParams(collective_id=0, has_side_effects=True, vmem_limit_bytes=60 << 20),
        name="whole",
    )(lengths.T, destination.reshape(1, TOK), keys, values, queries, grad_out)


def solution(mesh):
    rows = P(("dp", "ctx"), None)
    return jax.shard_map(
        local,
        mesh=mesh,
        in_specs=(rows, rows, rows, rows, P(("dp", "ctx")), P()),
        out_specs=(rows, rows, rows, rows),
        check_vma=False,
    )
```

time: 499 us -> 212 us (0.42); the launches traced: 490 us -> 212 us
  Pallas kernels: 0 us -> 206 us
  waiting for transfers between devices: 126 us -> 0 us
  local copies, waits for them, and re-layouts: 115 us -> 5.33 us
  matrix products: 105 us -> 0 us
  other arithmetic: 70.2 us -> 0 us
  starting transfers between devices: 59.3 us -> 0 us
  between operations: 14.3 us -> 0.65 us
    pallas_call x0 -> x1, Pallas kernels: none -> 206 us  [local(): pl.pallas_call(whole_kernel, out_shape=(jax.ShapeDtypeStruct((TOK, 4096),...]
    all_to_all x9 -> x0, waiting for transfers between devices: 126 us -> none  [the longest x1 34.7 us: local(): lax.all_to_all(to_owners(attended_rows), 'dp', split_axis=0, concat_axis=...]
    dot_general x14 -> x0, matrix products: 73.3 us -> none  [the longest x1 21 us: local(): jnp.einsum('grqk,qgrd->kgd', prob_b, d_heads, preferred_element_type=jnp....]
    all_to_all x9 -> x0, starting transfers between devices: 59 us -> none  [the longest x1 7.49 us: local(): lax.all_to_all(to_owners(attended_rows), 'dp', split_axis=0, concat_axis=...]
    gather x17 -> x0, local copies, waits for them, and re-layouts: 55.4 us -> none  [the longest x4 13.6 us: read_back(): return returned.reshape(n_dp * cap, -1)[slot_of]]
    dynamic_update_slice x4 -> x0, other arithmetic: 35.2 us -> none  [local(): prob_all, att_all = lax.map(forward_group, (q_groups, k_groups, v_groups))]
    sub x4 -> x0, matrix products: 32 us -> none  [forward_group(): expo = jnp.exp(masked - top)]
    convert_element_type x1 -> x0, other arithmetic: 20.9 us -> none  [local(): prob_b = prob_all.astype(jnp.bfloat16)]
  transfers between devices with their start and end apart: 12 -> 0, of which waited for: 8 -> 0; matrix products, arithmetic and copies ran while one was open for 16% -> 0% of each run, Pallas kernels for 0% -> 0%
where the time goes in v3:
time: 212 us
  Pallas kernels  206 us (97%)
  local copies, waits for them, and re-layouts  5.33 us (3%)
    pallas_call x1, Pallas kernels, local(): pl.pallas_call(whole_kernel, out_shape=(jax.ShapeDtypeStruct((TOK, 4096),...  206 us
    unnamed x10, local copies, waits for them, and re-layouts  5.33 us

profile of v3, /device:TPU:16, one launch (start us, length us, event | category | flops | bytes accessed | tf_op | source)
XLA Modules:
  0.0 212.1 jit_solution(7052958037269128086)
XLA Ops:
  0.6 206.1 %whole.1 = (bf16[192,4096]{1,0:T(8,128)(2,1)}, bf16[192,4096]{1,0:T(8,128)(2,1)}, bf16[192,512]{1,0:T(8,128)(2,1)}, bf16[192,512]{1,0:T(8,128)(2,1)}) custom-call(s32[2,16]{1,0:T(2,128)} %bitcast.2, s32[1,192]{1,0:T(1,128)} %bitcast.3, bf16[192,512]{1,0:T(8,128)(2,1)} %k_ref.1, bf16[192,512]{1,0:T(8,128)(2,1)} %v_ref.1, bf16[192,4096]{1,0:T(8,128)(2,1)} %qin_ref.1, ...), custom_call_target="tpu_custom_call" | custom-call | tf_op jit(solution)/shard_map/whole/pallas_call | solution.py:446
  206.8 0.0 copy-start
  206.8 2.8 %copy.14 = bf16[192,4096]{1,0:T(8,128)(2,1)} copy(bf16[192,4096]{1,0:T(8,128)(2,1)} %get-tuple-element.8) | data formatting | bytes 3145728
  209.6 0.0 copy-done
  209.6 0.0 copy-start.2
  209.6 0.0 copy-start.1
  209.6 1.1 copy.15
  210.8 0.0 copy-done.2
  210.8 0.7 copy.16
  211.4 0.0 copy-done.1
  211.4 0.7 copy.17
Async XLA Ops:
  206.8 2.8 %copy-start = (bf16[192,4096]{1,0:T(8,128)(2,1)S(1)}, bf16[192,4096]{1,0:T(8,128)(2,1)}, u32[]{:S(2)}) copy-start(bf16[192,4096]{1,0:T(8,128)(2,1)} %get-tuple-element.9) | copy-start | bytes 4718596
  209.6 1.1 copy-start.2
  209.6 1.8 copy-start.1
